TPU v7x, 256 devices: a whole 4x4x8 slice. The times are simulated.
256 devices in a mesh: dp: 16 (over z, y_lo), fsdp: 16 (over y_hi, x, core).
Axes of the slice: x: 4, y: 4 (y_hi: 2, y_lo: 2; y = y_hi * 2 + y_lo), z: 8, core: 2. Of those that a mesh axis runs over, the one named last changes fastest.
Arguments:
- tokens_in: bfloat16 [32768, 2560], P(('dp', 'fsdp')), may hold values from -6 to 6
- queries_first: bfloat16 [32768, 2560], P(('dp', 'fsdp')), may hold values from -6 to 6
- queries_second: bfloat16 [32768, 2560], P(('dp', 'fsdp')), may hold values from -6 to 6
- teacher_logits: bfloat16 [32768, 256], P(('dp', 'fsdp')), may hold values from -15 to 15
- rollout_lengths: int32 [16, 16, 32], P(None, 'fsdp'), may hold values from 1 to 12, as said below
- send_counts: int32 [16, 16, 16], P(None, 'fsdp'), may hold values from 1 to 3, as said below
- key_value_weight: bfloat16 [2560, 1024], P('fsdp'), may hold values from -0.125 to 0.125
- head_slice: bfloat16 [2560, 256], P('fsdp'), may hold values from -0.375 to 0.375
Outputs:
- input_grad: bfloat16 [32768, 2560], P(('dp', 'fsdp'))
- kv_grad: float32 [2560, 1024], P('fsdp')
- head_grad: float32 [2560, 256], P('fsdp')
Inputs may be any that keep to these rules, and one draw needn't show every extreme that they name: `rollout_lengths`: each device's rollout lengths sum to 128. The rollouts that one device sends to one group span at most 12 rows, exactly 12 for some group, and every device (d, f) receives exactly 128 rows in all. `send_counts`: for every device the counts sum to 32.
All inputs are finite; a program needn't handle non-finite values.
Results may differ from a plain program's by a relative error of at most 0.025.
Values may be sent and summed in bfloat16 or wider, within the bound.
A program may use at most 128 MiB of HBM per device.

v0:
```python
import jax
import jax.numpy as jnp
from jax import lax
from jax.sharding import PartitionSpec as P

KEY_VALUE_HEADS = 4
HEADS_PER_KEY = 5
HEAD_SIZE = 128


EPS = 1e-06


def pick(table, index):
    slots = jnp.arange(table.shape[-1], dtype=jnp.int32)
    match = (index[..., :, None] == slots).astype(jnp.int32)
    return jnp.sum(table[..., None, :] * match, -1)


def piece_bounds(lengths, counts):
    zero = jnp.zeros(lengths.shape[:-1] + (1,), jnp.int32)
    len_cum = jnp.concatenate([zero, jnp.cumsum(lengths, -1)], -1)
    count_end = jnp.cumsum(counts, -1)
    begin = pick(len_cum, count_end - counts)
    return (len_cum, begin, pick(len_cum, count_end) - begin)


def pack_rows(source_array, begin, size, width):
    slot = jnp.arange(width, dtype=jnp.int32)
    index = begin[:, None] + slot[None, :]
    keep = slot[None, :] < size[:, None]
    flat = jnp.minimum(index, source_array.shape[0] - 1).reshape(-1)
    taken = source_array[flat].reshape(index.shape + (source_array.shape[1],))
    return jnp.where(keep[..., None], taken, jnp.zeros((), source_array.dtype))


def arrival(size_in, packed_row_list, width):
    offset_end = jnp.cumsum(size_in)
    offset = offset_end - size_in
    position = jnp.arange(packed_row_list, dtype=jnp.int32)
    source = jnp.sum((position[:, None] >= offset_end[None, :]).astype(jnp.int32), 1)
    within = position - pick(offset[None, :], source[None, :])[0]
    return (source, within, source * width + within)


def unpack_rows(received, index):
    return received.reshape(-1, received.shape[-1])[index]


def attend(query, key_rows, value_rows, visible):
    scores = jnp.einsum(
        "qkgd,tkd->kgqt", query, key_rows, preferred_element_type=jnp.float32
    ) * HEAD_SIZE ** (-0.5)
    scores = jnp.where(visible, scores, -1e30)
    peak = jnp.max(scores, -1, keepdims=True)
    weights = jnp.exp(scores - peak)
    probs = weights / jnp.sum(weights, -1, keepdims=True)
    probs_b = probs.astype(jnp.bfloat16)
    out = jnp.einsum("kgqt,tkd->qkgd", probs_b, value_rows, preferred_element_type=jnp.float32)
    return (probs, probs_b, out)


def attend_back(query, value_rows, probs, probs_b, out, output_gradient):
    packed_row_list = query.shape[0]
    value_gradient = jnp.einsum(
        "kgqt,qkgd->tkd", probs_b, output_gradient, preferred_element_type=jnp.float32
    )
    grad_probs = jnp.einsum(
        "qkgd,tkd->kgqt", output_gradient, value_rows, preferred_element_type=jnp.float32
    )
    carry = jnp.einsum("qkgd,qkgd->kgq", output_gradient.astype(jnp.float32), out)
    grad_scores = (probs * (grad_probs - carry[..., None]) * HEAD_SIZE ** (-0.5)).astype(
        jnp.bfloat16
    )
    key_gradient = jnp.einsum(
        "kgqt,qkgd->tkd", grad_scores, query, preferred_element_type=jnp.float32
    )
    joined_rows = jnp.concatenate(
        [
            key_gradient.reshape(packed_row_list, KEY_VALUE_HEADS * HEAD_SIZE),
            value_gradient.reshape(packed_row_list, KEY_VALUE_HEADS * HEAD_SIZE),
        ],
        1,
    )
    return joined_rows.astype(jnp.bfloat16)


def pair_pass(tokens, first_layer, second_layer, teacher, segment, w_full, head_full):
    packed_row_list = tokens.shape[0]
    position = jnp.arange(packed_row_list, dtype=jnp.int32)
    visible = (segment[:, None] == segment[None, :]) & (position[None, :] <= position[:, None])
    key_value_rows = jnp.dot(tokens, w_full, preferred_element_type=jnp.float32).astype(
        jnp.bfloat16
    )
    key_rows = key_value_rows[:, : KEY_VALUE_HEADS * HEAD_SIZE].reshape(
        packed_row_list, KEY_VALUE_HEADS, HEAD_SIZE
    )
    value_rows = key_value_rows[:, KEY_VALUE_HEADS * HEAD_SIZE :].reshape(
        packed_row_list, KEY_VALUE_HEADS, HEAD_SIZE
    )
    query_upper = first_layer.reshape(packed_row_list, KEY_VALUE_HEADS, HEADS_PER_KEY, HEAD_SIZE)
    query_lower = second_layer.reshape(packed_row_list, KEY_VALUE_HEADS, HEADS_PER_KEY, HEAD_SIZE)
    probs_a, probs_ab, out_a = attend(query_upper, key_rows, value_rows, visible)
    probs_b, probs_bb, out_b = attend(query_lower, key_rows, value_rows, visible)
    width = tokens.shape[1]
    hidden = (
        tokens.astype(jnp.float32)
        + out_a.reshape(packed_row_list, width)
        + out_b.reshape(packed_row_list, width)
    )
    inverse = lax.rsqrt(jnp.mean(hidden * hidden, -1, keepdims=True) + EPS)
    normed = hidden * inverse
    normed_b = normed.astype(jnp.bfloat16)
    logits = jnp.dot(normed_b, head_full, preferred_element_type=jnp.float32)
    student = jax.nn.log_softmax(logits, -1)
    target = jax.nn.log_softmax(teacher.astype(jnp.float32), -1)
    grad_logits = (jnp.exp(student) - jnp.exp(target)).astype(jnp.bfloat16)
    grad_normed = lax.dot_general(
        grad_logits, head_full, (((1,), (1,)), ((), ())), preferred_element_type=jnp.float32
    )
    hidden_gradient = inverse * (
        grad_normed - normed * jnp.mean(grad_normed * normed, -1, keepdims=True)
    )
    output_gradient = hidden_gradient.astype(jnp.bfloat16).reshape(
        packed_row_list, KEY_VALUE_HEADS, HEADS_PER_KEY, HEAD_SIZE
    )
    kv_a = attend_back(query_upper, value_rows, probs_a, probs_ab, out_a, output_gradient)
    kv_b = attend_back(query_lower, value_rows, probs_b, probs_bb, out_b, output_gradient)
    back_a = lax.dot_general(
        kv_a, w_full, (((1,), (1,)), ((), ())), preferred_element_type=jnp.float32
    )
    back_b = lax.dot_general(
        kv_b, w_full, (((1,), (1,)), ((), ())), preferred_element_type=jnp.float32
    )
    grad_rows = (hidden_gradient + back_a + back_b).astype(jnp.bfloat16)
    return (grad_rows, kv_a, kv_b, normed_b, grad_logits)


def on_device(
    tokens_in,
    queries_first,
    queries_second,
    teacher_logits,
    rollout_lengths,
    send_counts,
    key_value_weight,
    head_slice,
):
    groups = lax.axis_size("dp")
    here = lax.axis_index("dp")
    packed_row_list = tokens_in.shape[0]
    width = 3 * packed_row_list // (2 * groups)
    lengths = rollout_lengths[:, 0, :]
    counts = send_counts[:, 0, :]
    len_cum, begin, size = piece_bounds(lengths, counts)
    my_begin = lax.dynamic_index_in_dim(begin, here, 0, keepdims=False)
    my_size = lax.dynamic_index_in_dim(size, here, 0, keepdims=False)
    size_in = lax.dynamic_index_in_dim(size, here, 1, keepdims=False)
    begin_in = lax.dynamic_index_in_dim(begin, here, 1, keepdims=False)
    w_full, head_full = (
        lax.all_gather(key_value_weight, "fsdp", axis=0, tiled=True),
        lax.all_gather(head_slice, "fsdp", axis=0, tiled=True),
    )
    send_tokens = pack_rows(tokens_in, my_begin, my_size, width)
    send_first = pack_rows(queries_first, my_begin, my_size, width)
    send_second = pack_rows(queries_second, my_begin, my_size, width)
    send_teacher = pack_rows(teacher_logits, my_begin, my_size, width)
    got_tokens, got_first, got_second, got_teacher = (
        lax.all_to_all(send_tokens, "dp", split_axis=0, concat_axis=0, tiled=True),
        lax.all_to_all(send_first, "dp", split_axis=0, concat_axis=0, tiled=True),
        lax.all_to_all(send_second, "dp", split_axis=0, concat_axis=0, tiled=True),
        lax.all_to_all(send_teacher, "dp", split_axis=0, concat_axis=0, tiled=True),
    )
    source, within, index = arrival(size_in, packed_row_list, width)
    tokens = unpack_rows(got_tokens, index)
    first_layer = unpack_rows(got_first, index)
    second_layer = unpack_rows(got_second, index)
    teacher = unpack_rows(got_teacher, index)
    source_row = pick(begin_in[None, :], source[None, :])[0] + within
    chosen = (source[:, None] == jnp.arange(groups, dtype=jnp.int32)[None, :]).astype(jnp.int32)
    bounds = jnp.sum(chosen[:, :, None] * len_cum[None, :, :], 1)
    rollout = jnp.sum((source_row[:, None] >= bounds[:, 1:]).astype(jnp.int32), 1)
    segment = source * lengths.shape[1] + rollout
    grad_rows, kv_a, kv_b, normed_b, grad_logits = pair_pass(
        tokens, first_layer, second_layer, teacher, segment, w_full, head_full
    )
    part = tokens
    first_term = lax.dot_general(
        part, kv_a, (((0,), (0,)), ((), ())), preferred_element_type=jnp.float32
    )
    second_term = lax.dot_general(
        part, kv_b, (((0,), (0,)), ((), ())), preferred_element_type=jnp.float32
    )
    kv_shard = lax.psum_scatter(
        (first_term + second_term).astype(jnp.bfloat16), "fsdp", scatter_dimension=0, tiled=True
    )
    part = normed_b
    head_shard = lax.psum_scatter(
        lax.dot_general(
            part, grad_logits, (((0,), (0,)), ((), ())), preferred_element_type=jnp.float32
        ).astype(jnp.bfloat16),
        "fsdp",
        scatter_dimension=0,
        tiled=True,
    )
    kv_total, head_total = (
        lax.psum(kv_shard, "dp").astype(jnp.float32),
        lax.psum(head_shard, "dp").astype(jnp.float32),
    )
    return (grad_rows, kv_total, head_total)


def solution(mesh):
    in_specs = (
        P(("dp", "fsdp"), None),
        P(("dp", "fsdp"), None),
        P(("dp", "fsdp"), None),
        P(("dp", "fsdp"), None),
        P(None, "fsdp", None),
        P(None, "fsdp", None),
        P("fsdp", None),
        P("fsdp", None),
    )
    out_specs = (P(("dp", "fsdp"), None), P("fsdp", None), P("fsdp", None))
    return jax.shard_map(
        on_device, mesh=mesh, in_specs=in_specs, out_specs=out_specs, check_vma=False
    )
```

profile of v0, /device:TPU:2, one launch (start us, length us, event | category | flops | bytes accessed | tf_op | source)
XLA Modules:
  0.0 494.6 jit_solution(1406884428596253666)
XLA Ops:
  14.0 9.6 %all-to-all-start.3 = ((bf16[16,12,256]{2,1,0:T(8,128)(2,1)}), bf16[16,12,256]{2,1,0:T(8,128)(2,1)S(1)}, u32[]{:S(2)}, u32[]{:S(2)}) async-start(bf16[16,12,256]{2,1,0:T(8,128)(2,1)} %broadcast_select_fusion.3), calls=%async_computation.3 | async-start | bytes 262144 | tf_op jit(solution)/shard_map/all_to_all | solution.py:172
  30.7 3.5 broadcast_select_fusion.1
  34.3 42.2 %all_to_all.20 = bf16[16,12,2560]{2,1,0:T(8,128)(2,1)} all-to-all(bf16[16,12,2560]{2,1,0:T(8,128)(2,1)S(1)} %get-tuple-element.14), channel_id=1, replica_groups=mesh['dp'=16,'fsdp'=16] {'dp'}, dimensions={0} | all-to-all | bytes 1966080 | tf_op jit(solution)/shard_map/all_to_all | solution.py:170
  76.4 3.7 all-to-all-start.2
  81.2 30.8 %all-to-all-done.2 = bf16[16,12,2560]{2,1,0:T(8,128)(2,1)S(1)} async-done(((bf16[16,12,2560]{2,1,0:T(8,128)(2,1)}), bf16[16,12,2560]{2,1,0:T(8,128)(2,1)S(1)}, u32[]{:S(2)}, u32[]{:S(2)}) %all-to-all-start.2) | async-done | bytes 983072 | tf_op jit(solution)/shard_map/all_to_all | solution.py:171
  112.0 4.4 all-to-all-start
  124.3 23.5 %all-to-all-done = bf16[16,12,2560]{2,1,0:T(8,128)(2,1)} async-done(((bf16[16,12,2560]{2,1,0:T(8,128)(2,1)}), bf16[16,12,2560]{2,1,0:T(8,128)(2,1)}, u32[]{:S(2)}, u32[]{:S(2)}) %all-to-all-start) | async-done | bytes 983072 | tf_op jit(solution)/shard_map/all_to_all | solution.py:169
  151.5 3.4 convolution_convert_fusion.1
  157.8 2.8 fusion.108
  160.6 3.5 fusion.24
  164.1 2.8 copy.88
  175.3 2.2 copy.89
  177.9 2.6 convolution_bitcast_fusion
  180.4 3.1 fusion.29
  183.5 3.7 fusion.30
  187.3 2.8 fusion.27
  190.1 2.1 fusion.28
  192.2 2.5 fusion.40
  194.7 3.9 add_convert_fusion
  199.6 5.6 %convolution_add_fusion.1 = f32[128,2560]{1,0:T(8,128)} fusion(bf16[2560,1024]{1,0:T(8,128)(2,1)} %all-gather.3.cloned.1.call-done, bf16[128,512]{0,1:T(8,128)(2,1)S(1)} %bitcast.175, bf16[128,512]{0,1:T(8,128)(2,1)S(1)} %bitcast.173, f32[128,2560]{1,0:T(8,128)S(1)} %get-tuple-element.26, f32[128,2560]{1,0:T(8,128)S(1)} %add_multiply_fusion, ...), kind=kOutput, calls=%fused_computation.15 | convolution fusion | flops 672923648 | bytes 9438208 | tf_op jit(solution)/shard_map/dot_general | solution.py:129
  205.2 45.8 %reduce-scatter.5.cloned.1.call-done = bf16[160,256]{1,0:T(8,128)(2,1)} async-done(((bf16[2560,256]{1,0:T(8,128)(2,1)}), bf16[160,256]{1,0:T(8,128)(2,1)}) %reduce-scatter.5.cloned.1.call-update) | async-done | bytes 81936 | tf_op jit(solution)/shard_map/reduce_scatter | solution.py:198
  251.0 96.1 %reduce-scatter.3.cloned.1.call-done = bf16[160,1024]{1,0:T(8,128)(2,1)} async-done(((bf16[2560,1024]{1,0:T(8,128)(2,1)}), bf16[160,1024]{1,0:T(8,128)(2,1)}) %reduce-scatter.3.cloned.1.call-update) | async-done | bytes 327696 | tf_op jit(solution)/shard_map/reduce_scatter | solution.py:194
  347.1 5.6 %fusion.4 = bf16[128,2560]{1,0:T(8,128)(2,1)} fusion(f32[128,2560]{1,0:T(8,128)} %convolution_add_fusion.1, bf16[2560,1024]{1,0:T(8,128)(2,1)} %all-gather.3.cloned.1.call-done, bf16[128,512]{0,1:T(8,128)(2,1)S(1)} %bitcast.171, bf16[128,512]{0,1:T(8,128)(2,1)S(1)} %bitcast.169), kind=kOutput, calls=%fused_computation.16 | convolution fusion | flops 672268288 | bytes 7471104 | tf_op jit(solution)/shard_map/dot_general | solution.py:132
  352.7 131.9 %all-reduce.4.cloned.1.call-done = (bf16[160,1024]{1,0:T(8,128)(2,1)}, bf16[160,256]{1,0:T(8,128)(2,1)}) async-done(((bf16[160,1024]{1,0:T(8,128)(2,1)}, bf16[160,256]{1,0:T(8,128)(2,1)}), (bf16[160,1024]{1,0:T(8,128)(2,1)}, bf16[160,256]{1,0:T(8,128)(2,1)})) %all-reduce.4.cloned.1.call-update) | async-done | bytes 409616 | tf_op jit(solution)/shard_map/psum | solution.py:207
  (112 shorter events, 42.4 us)
Async XLA Ops:
  7.2 16.4 %copy-start = (bf16[128,2560]{1,0:T(8,128)(2,1)S(1)}, bf16[128,2560]{1,0:T(8,128)(2,1)}, u32[]{:S(2)}) copy-start(bf16[128,2560]{1,0:T(8,128)(2,1)} %param.11) | copy-start | bytes 1966084
  7.2 144.3 %all-gather.3.cloned.1.call-start = ((), (), s32[]{:S(2)}) async-start(), calls=%async_computation.6 | async-start | bytes 5570560 | tf_op jit(solution)/shard_map/all_gather | solution.py:161
  14.0 20.3 %all-to-all-start.3 = ((bf16[16,12,256]{2,1,0:T(8,128)(2,1)}), bf16[16,12,256]{2,1,0:T(8,128)(2,1)S(1)}, u32[]{:S(2)}, u32[]{:S(2)}) async-start(bf16[16,12,256]{2,1,0:T(8,128)(2,1)} %broadcast_select_fusion.3), calls=%async_computation.3 | async-start | bytes 262144 | tf_op jit(solution)/shard_map/all_to_all | solution.py:172
  24.8 1.1 copy-start.2
  27.1 1.2 copy-start.3
  76.4 35.6 %all-to-all-start.2 = ((bf16[16,12,2560]{2,1,0:T(8,128)(2,1)}), bf16[16,12,2560]{2,1,0:T(8,128)(2,1)S(1)}, u32[]{:S(2)}, u32[]{:S(2)}) async-start(bf16[16,12,2560]{2,1,0:T(8,128)(2,1)} %get-tuple-element.15), calls=%async_computation.2 | async-start | bytes 2621440 | tf_op jit(solution)/shard_map/all_to_all | solution.py:171
  80.1 88.3 %all-gather.5.cloned.1.call-start = ((), (), s32[]{:S(2)}) async-start(), calls=%async_computation.7 | async-start | bytes 1392640 | tf_op jit(solution)/shard_map/all_gather | solution.py:162
  112.0 35.7 %all-to-all-start = ((bf16[16,12,2560]{2,1,0:T(8,128)(2,1)}), bf16[16,12,2560]{2,1,0:T(8,128)(2,1)}, u32[]{:S(2)}, u32[]{:S(2)}) async-start(bf16[16,12,2560]{2,1,0:T(8,128)(2,1)} %get-tuple-element.16), calls=%async_computation | async-start | bytes 2621440 | tf_op jit(solution)/shard_map/all_to_all | solution.py:169
  116.4 134.5 %reduce-scatter.5.cloned.1.call-start = ((), (), s32[]{:S(2)}) async-start(), calls=%async_computation.9 | async-start | bytes 1392640 | tf_op jit(solution)/shard_map/reduce_scatter | solution.py:198
  151.5 3.5 copy-start.5
  154.9 1.7 copy-start.10
  155.0 5.6 %copy-start.8 = (bf16[128,4,128]{2,1,0:T(4,128)(2,1)}, bf16[128,4,128]{2,1,0:T(4,128)(2,1)S(1)}, u32[]{:S(2)}) copy-start(bf16[128,4,128]{2,1,0:T(4,128)(2,1)S(1)} %reshape.384) | copy-start | bytes 393220
  157.4 3.2 copy-start.4
  160.6 19.9 %copy-start.15 = (f32[4,5,128]{2,1,0:T(8,128)}, f32[4,5,128]{2,1,0:T(8,128)S(1)}, u32[]{:S(2)}) copy-start(f32[4,5,128]{2,1,0:T(8,128)S(1)} %get-tuple-element.17) | copy-start | bytes 30724
  166.9 7.3 %copy-start.11 = (f32[128]{0:T(128)}, f32[128]{0:T(128)S(1)}, u32[]{:S(2)}) copy-start(f32[128]{0:T(128)S(1)} %add_rsqrt_fusion) | copy-start | bytes 1540
  174.1 1.2 copy-start.13
  175.3 2.5 copy-start.9
  177.6 169.4 %reduce-scatter.3.cloned.1.call-start = ((), (), s32[]{:S(2)}) async-start(), calls=%async_computation.8 | async-start | bytes 5570560 | tf_op jit(solution)/shard_map/reduce_scatter | solution.py:194
  198.7 0.9 copy-start.6
  198.7 1.0 copy-start.7
  198.7 1.0 copy-start.12
  198.7 1.0 copy-start.14
  198.7 285.9 %all-reduce.4.cloned.1.call-start = ((), (), s32[]{:S(2)}) async-start(), calls=%async_computation.10 | async-start | bytes 819200 | tf_op jit(solution)/shard_map/psum | solution.py:207
  347.1 141.0 %copy-start.1 = (bf16[128,2560]{1,0:T(8,128)(2,1)S(1)}, bf16[128,2560]{1,0:T(8,128)(2,1)}, u32[]{:S(2)}) copy-start(bf16[128,2560]{1,0:T(8,128)(2,1)} %param.11) | copy-start | bytes 1966084
Sparse Core Ops, SparseCore 0:
  10.7 77.8 all-gather.2
  91.4 54.3 all-gather.4
  177.7 73.2 reduce-scatter.4
  255.2 91.7 reduce-scatter.2
  349.6 134.9 all-reduce.3
where the time goes:
time: 496 us; the launch traced here: 495 us
  waiting for transfers between devices  329 us (66%)
  matrix products  49.4 us (10%)
  blocking collectives  42.2 us (9%)
  local copies, waits for them, and re-layouts  26.2 us (5%)
  starting transfers between devices  18.3 us (4%)
  other arithmetic  15 us (3%)
  between operations  14.2 us (3%)
    psum x1, waiting for transfers between devices, on_device(): lax.psum(kv_shard, 'dp').astype(jnp.float32)  132 us
    reduce_scatter x1, waiting for transfers between devices, on_device(): lax.psum_scatter((first_term + second_term).astype(jnp.bfloat16), 'fsdp',...  96.1 us
    reduce_scatter x1, waiting for transfers between devices, on_device(): lax.psum_scatter(lax.dot_general(part, grad_logits, (((0,), (0,)), ((), (...  45.8 us
    all_to_all x1, blocking collectives, on_device(): lax.all_to_all(send_first, 'dp', split_axis=0, concat_axis=0, tiled=True)  42.2 us
    all_to_all x1, waiting for transfers between devices, on_device(): lax.all_to_all(send_second, 'dp', split_axis=0, concat_axis=0, tiled=True)  30.8 us
    all_to_all x1, waiting for transfers between devices, on_device(): lax.all_to_all(send_tokens, 'dp', split_axis=0, concat_axis=0, tiled=True)  23.5 us
  transfers between devices with their start and end apart: 8, of which 5 were waited for; matrix products, arithmetic and copies ran while one was open for 15% of the time, Pallas kernels for 0%

commit v1 on v0

--- a/solution.py
+++ b/solution.py
@@ -156,34 +156,21 @@
     my_begin = lax.dynamic_index_in_dim(begin, here, 0, keepdims=False)
     my_size = lax.dynamic_index_in_dim(size, here, 0, keepdims=False)
     size_in = lax.dynamic_index_in_dim(size, here, 1, keepdims=False)
-    begin_in = lax.dynamic_index_in_dim(begin, here, 1, keepdims=False)
     w_full, head_full = (
         lax.all_gather(key_value_weight, "fsdp", axis=0, tiled=True),
         lax.all_gather(head_slice, "fsdp", axis=0, tiled=True),
     )
-    send_tokens = pack_rows(tokens_in, my_begin, my_size, width)
-    send_first = pack_rows(queries_first, my_begin, my_size, width)
-    send_second = pack_rows(queries_second, my_begin, my_size, width)
-    send_teacher = pack_rows(teacher_logits, my_begin, my_size, width)
-    got_tokens, got_first, got_second, got_teacher = (
-        lax.all_to_all(send_tokens, "dp", split_axis=0, concat_axis=0, tiled=True),
-        lax.all_to_all(send_first, "dp", split_axis=0, concat_axis=0, tiled=True),
-        lax.all_to_all(send_second, "dp", split_axis=0, concat_axis=0, tiled=True),
-        lax.all_to_all(send_teacher, "dp", split_axis=0, concat_axis=0, tiled=True),
-    )
+    own_ends = lax.dynamic_index_in_dim(len_cum, here, 0, keepdims=False)[1:]
+    position = jnp.arange(packed_row_list, dtype=jnp.int32)
+    segment = jnp.sum((position[:, None] >= own_ends[None, :]).astype(jnp.int32), 1)
+    tokens = tokens_in
+    grad_rows, kv_a, kv_b, normed_b, grad_logits = pair_pass(
+        tokens, queries_first, queries_second, teacher_logits, segment, w_full, head_full
+    )
+    send_rows = pack_rows(grad_rows, my_begin, my_size, width)
+    got_rows = lax.all_to_all(send_rows, "dp", split_axis=0, concat_axis=0, tiled=True)
     source, within, index = arrival(size_in, packed_row_list, width)
-    tokens = unpack_rows(got_tokens, index)
-    first_layer = unpack_rows(got_first, index)
-    second_layer = unpack_rows(got_second, index)
-    teacher = unpack_rows(got_teacher, index)
-    source_row = pick(begin_in[None, :], source[None, :])[0] + within
-    chosen = (source[:, None] == jnp.arange(groups, dtype=jnp.int32)[None, :]).astype(jnp.int32)
-    bounds = jnp.sum(chosen[:, :, None] * len_cum[None, :, :], 1)
-    rollout = jnp.sum((source_row[:, None] >= bounds[:, 1:]).astype(jnp.int32), 1)
-    segment = source * lengths.shape[1] + rollout
-    grad_rows, kv_a, kv_b, normed_b, grad_logits = pair_pass(
-        tokens, first_layer, second_layer, teacher, segment, w_full, head_full
-    )
+    grad_rows = unpack_rows(got_rows, index)
     part = tokens
     first_term = lax.dot_general(
         part, kv_a, (((0,), (0,)), ((), ())), preferred_element_type=jnp.float32

time: 496 us -> 498 us (level)
  waiting for transfers between devices: 329 us -> 393 us
  blocking collectives: 42.2 us -> 0 us
  starting transfers between devices: 18.3 us -> 7.54 us
    reduce_scatter x1 -> x0, waiting for transfers between devices: 96.1 us -> none  [on_device(): lax.psum_scatter((first_term + second_term).astype(jnp.bfloat16), 'fsdp',...]
    unnamed x5 -> x6, waiting for transfers between devices: 1.43 us -> 78.1 us
    all_gather x1, waiting for transfers between devices: 0.01 us -> 63.9 us  [on_device(): lax.all_gather(key_value_weight, 'fsdp', axis=0, tiled=True)]
    all_to_all x3 -> x1, waiting for transfers between devices: 54.3 us -> 0.01 us  [on_device(): lax.all_to_all(send_rows, 'dp', split_axis=0, concat_axis=0, tiled=True)]
    all_to_all x1 -> x0, blocking collectives: 42.2 us -> none  [on_device(): lax.all_to_all(send_first, 'dp', split_axis=0, concat_axis=0, tiled=True)]
    all_gather x1, waiting for transfers between devices: 0.02 us -> 36.3 us  [on_device(): lax.all_gather(head_slice, 'fsdp', axis=0, tiled=True)]
    reduce_scatter x1, waiting for transfers between devices: 45.8 us -> 76.3 us  [on_device(): lax.psum_scatter(lax.dot_general(part, grad_logits, (((0,), (0,)), ((), (...]
    unnamed x32 -> x43, local copies, waits for them, and re-layouts: 1.79 us -> 16.6 us
  transfers between devices with their start and end apart: 8 -> 6, of which waited for: 5 -> 5; matrix products, arithmetic and copies ran while one was open for 15% -> 8% of each run, Pallas kernels for 0% -> 0%
where the time goes in v1:
time: 498 us
  waiting for transfers between devices  393 us (79%)
  matrix products  45.9 us (9%)
  local copies, waits for them, and re-layouts  26.9 us (5%)
  between operations  14.1 us (3%)
  other arithmetic  10.2 us (2%)
  starting transfers between devices  7.54 us (2%)
    psum x1, waiting for transfers between devices, on_device(): lax.psum(kv_shard, 'dp').astype(jnp.float32)  138 us
    unnamed x6, waiting for transfers between devices  78.1 us
    reduce_scatter x1, waiting for transfers between devices, on_device(): lax.psum_scatter(lax.dot_general(part, grad_logits, (((0,), (0,)), ((), (...  76.3 us
    all_gather x1, waiting for transfers between devices, on_device(): lax.all_gather(key_value_weight, 'fsdp', axis=0, tiled=True)  63.9 us
    all_gather x1, waiting for transfers between devices, on_device(): lax.all_gather(head_slice, 'fsdp', axis=0, tiled=True)  36.3 us
    unnamed x43, local copies, waits for them, and re-layouts  16.6 us
  transfers between devices with their start and end apart: 6, of which 5 were waited for; matrix products, arithmetic and copies ran while one was open for 8% of the time, Pallas kernels for 0%

profile of v1, /device:TPU:2, one launch (start us, length us, event | category | flops | bytes accessed | tf_op | source)
XLA Modules:
  0.0 497.5 jit_solution(9107354183706292935)
XLA Ops:
  11.8 2.2 copy.95
  14.5 63.9 %all-gather.3.cloned.1.call-done = bf16[2560,1024]{1,0:T(8,128)(2,1)} async-done(((bf16[160,1024]{1,0:T(8,128)(2,1)}), bf16[2560,1024]{1,0:T(8,128)(2,1)}) %all-gather.3.cloned.1.call-update) | async-done | bytes 5242896 | tf_op jit(solution)/shard_map/all_gather | solution.py:160
  78.5 3.3 convolution_convert_fusion.1
  85.4 3.4 fusion.107
  94.8 36.3 %all-gather.5.cloned.1.call-done = bf16[2560,256]{1,0:T(8,128)(2,1)} async-done(((bf16[160,256]{1,0:T(8,128)(2,1)}), bf16[2560,256]{1,0:T(8,128)(2,1)}) %all-gather.5.cloned.1.call-update) | async-done | bytes 1310736 | tf_op jit(solution)/shard_map/all_gather | solution.py:161
  131.1 1.9 fusion.110
  135.0 2.2 copy.107
  137.1 2.8 fusion.26
  139.9 2.8 fusion.27
  142.7 2.6 convolution_bitcast_fusion
  145.2 3.7 fusion.28
  149.0 3.7 fusion.29
  152.7 2.5 fusion.36
  155.2 3.9 fusion.4
  159.1 7.9 %copy.159 = bf16[2560,1024]{1,0:T(8,128)(2,1)} copy(bf16[2560,1024]{0,1:T(8,128)(2,1)} %fusion.4) | data formatting | bytes 10485760
  169.0 4.5 convolution_add_fusion.1
  173.5 4.4 fusion.5
  177.9 2.2 gather_fusion
  184.4 7.2 %all-to-all-start = ((bf16[16,12,2560]{2,1,0:T(8,128)(2,1)}), bf16[16,12,2560]{2,1,0:T(8,128)(2,1)S(1)}, u32[]{:S(2)}, u32[]{:S(2)}) async-start(bf16[16,12,2560]{2,1,0:T(8,128)(2,1)} %broadcast_select_fusion), calls=%async_computation | async-start | bytes 2621440 | tf_op jit(solution)/shard_map/all_to_all | solution.py:171
  192.0 76.7 %reduce-scatter.7.cloned.1.call-done = bf16[160,1024]{1,0:T(8,128)(2,1)} async-done(((bf16[2560,1024]{1,0:T(8,128)(2,1)}), bf16[160,1024]{1,0:T(8,128)(2,1)}) %reduce-scatter.7.cloned.1.call-update) | async-done | bytes 327696
  268.7 2.0 copy.160
  270.7 76.3 %reduce-scatter.5.cloned.1.call-done = bf16[160,256]{1,0:T(8,128)(2,1)} async-done(((bf16[2560,256]{1,0:T(8,128)(2,1)}), bf16[160,256]{1,0:T(8,128)(2,1)}) %reduce-scatter.5.cloned.1.call-update) | async-done | bytes 81936 | tf_op jit(solution)/shard_map/reduce_scatter | solution.py:185
  349.3 138.1 %all-reduce.4.cloned.1.call-done = (bf16[160,1024]{0,1:T(8,128)(2,1)}, bf16[160,256]{1,0:T(8,128)(2,1)}) async-done(((bf16[160,1024]{0,1:T(8,128)(2,1)}, bf16[160,256]{1,0:T(8,128)(2,1)}), (bf16[160,1024]{0,1:T(8,128)(2,1)}, bf16[160,256]{1,0:T(8,128)(2,1)})) %all-reduce.4.cloned.1.call-update) | async-done | bytes 409616 | tf_op jit(solution)/shard_map/psum | solution.py:194
  487.4 2.1 copy.114
  (99 shorter events, 26.9 us)
Async XLA Ops:
  7.2 6.9 %copy-start.5 = (bf16[128,2560]{1,0:T(8,128)(2,1)S(1)}, bf16[128,2560]{1,0:T(8,128)(2,1)}, u32[]{:S(2)}) copy-start(bf16[128,2560]{1,0:T(8,128)(2,1)} %param.11) | copy-start | bytes 1966084
  7.2 71.3 %all-gather.3.cloned.1.call-start = ((), (), s32[]{:S(2)}) async-start(), calls=%async_computation.3 | async-start | bytes 5570560 | tf_op jit(solution)/shard_map/all_gather | solution.py:160
  7.9 123.2 %all-gather.5.cloned.1.call-start = ((), (), s32[]{:S(2)}) async-start(), calls=%async_computation.4 | async-start | bytes 1392640 | tf_op jit(solution)/shard_map/all_gather | solution.py:161
  8.7 260.1 %reduce-scatter.7.cloned.1.call-start = ((), (), s32[]{:S(2)}) async-start(), calls=%async_computation.6 | async-start | bytes 5570560
  11.8 66.6 %copy-start = (bf16[128,2560]{1,0:T(8,128)(2,1)S(1)}, bf16[128,2560]{1,0:T(8,128)(2,1)}, u32[]{:S(2)}) copy-start(bf16[128,2560]{1,0:T(8,128)(2,1)} %param.9) | copy-start | bytes 1966084
  14.4 69.2 %copy-start.6 = (bf16[128,2560]{0,1:T(8,128)(2,1)}, bf16[128,2560]{0,1:T(8,128)(2,1)S(1)}, u32[]{:S(2)}) copy-start(bf16[128,2560]{0,1:T(8,128)(2,1)S(1)} %copy.101) | copy-start | bytes 1966084
  14.5 69.1 %copy-start.16 = (pred[128,128]{0,1:T(8,128)(4,1)}, pred[128,128]{0,1:T(8,128)(4,1)S(1)}, u32[]{:S(2)}) copy-start(pred[128,128]{0,1:T(8,128)(4,1)S(1)} %fusion.50) | copy-start | bytes 49156
  81.9 6.9 %copy-start.14 = (bf16[128,4,128]{2,1,0:T(4,128)(2,1)}, bf16[128,4,128]{2,1,0:T(4,128)(2,1)S(1)}, u32[]{:S(2)}) copy-start(bf16[128,4,128]{2,1,0:T(4,128)(2,1)S(1)} %reshape.265) | copy-start | bytes 393220
  81.9 6.8 %copy-start.13 = (bf16[128,4,128]{2,1,0:T(4,128)(2,1)}, bf16[128,4,128]{2,1,0:T(4,128)(2,1)S(1)}, u32[]{:S(2)}) copy-start(bf16[128,4,128]{2,1,0:T(4,128)(2,1)S(1)} %reshape.264) | copy-start | bytes 393220
  83.5 0.7 copy-start.18
  84.3 1.1 copy-start.3
  90.6 1.1 copy-start.2
  131.1 2.1 copy-start.1
  131.1 2.1 copy-start.4
  135.0 2.2 copy-start.17
  152.7 2.5 copy-start.7
  152.7 2.5 copy-start.10
  167.0 1.9 copy-start.9
  167.0 1.9 copy-start.12
  167.1 180.0 %reduce-scatter.5.cloned.1.call-start = ((), (), s32[]{:S(2)}) async-start(), calls=%async_computation.5 | async-start | bytes 1392640 | tf_op jit(solution)/shard_map/reduce_scatter | solution.py:185
  169.0 4.5 copy-start.8
  169.0 4.5 copy-start.11
  184.4 162.8 %all-to-all-start = ((bf16[16,12,2560]{2,1,0:T(8,128)(2,1)}), bf16[16,12,2560]{2,1,0:T(8,128)(2,1)S(1)}, u32[]{:S(2)}, u32[]{:S(2)}) async-start(bf16[16,12,2560]{2,1,0:T(8,128)(2,1)} %broadcast_select_fusion), calls=%async_computation | async-start | bytes 2621440 | tf_op jit(solution)/shard_map/all_to_all | solution.py:171
  191.5 295.9 %all-reduce.4.cloned.1.call-start = ((), (), s32[]{:S(2)}) async-start(), calls=%async_computation.7 | async-start | bytes 1212416 | tf_op jit(solution)/shard_map/psum | solution.py:194
  (1 other events, 0.7 us)
Sparse Core Ops, SparseCore 0:
  10.7 67.6 all-gather.2
  81.2 49.8 all-gather.4
  167.2 101.4 reduce-scatter.6
  272.7 74.2 reduce-scatter.4
  350.1 137.2 all-reduce.3

commit v2 on v1

v2 whole, which is shorter than its diff:
```python
import functools

import jax
import jax.numpy as jnp
from jax import lax
from jax.experimental import pallas as pl
from jax.experimental.pallas import tpu as pltpu
from jax.sharding import PartitionSpec as P

ROWS = 128
WIDTH = 2560
HEADS = 20
KV_HEADS = 4
PER_KEY = 5
D = 128
KV = 1024
VOCAB = 256
SHARD = 160
HALF = 80
Z = 8
EPS = 1e-06
SCALE = D ** (-0.5)
LOG2E = 1.4426950408889634
MESH = pl.DeviceIdType.MESH
F32 = jnp.float32
BF16 = jnp.bfloat16
COPIES = 160


def iota(shape, dim):
    return lax.broadcasted_iota(jnp.int32, shape, dim)


def dot(a, b):
    return jnp.dot(a, b, preferred_element_type=F32)


def dot_nt(a, b):
    return lax.dot_general(a, b, (((1,), (1,)), ((), ())), preferred_element_type=F32)


def lanes(block, size=D):
    return pl.ds(pl.multiple_of(block * D, D), size)


def rows_at(start, size, unit=16):
    return pl.ds(pl.multiple_of(start, unit), size)


class Wires:
    def __init__(self, send, recv, here):
        self.send, self.recv, self.here = send, recv, here
        self.count = 0
        self.open = []

    def start(self, src, dst, to):
        n = self.count
        self.count += 1
        copy = pltpu.make_async_remote_copy(
            src_ref=src, dst_ref=dst, send_sem=self.send.at[n], recv_sem=self.recv.at[n],
            device_id=to, device_id_type=MESH,
        )
        copy.start()
        self.open.append(copy)
        return n

    def arrived(self, n, landed):
        pltpu.make_async_remote_copy(
            src_ref=landed, dst_ref=landed, send_sem=self.send.at[n], recv_sem=self.recv.at[n],
            device_id=self.here, device_id_type=MESH,
        ).wait_recv()

    def drain(self):
        for copy in self.open:
            copy.wait_send()


def kernel(
    tok_h, q1_h, q2_h, tea_h, len_ref, cnt_ref, w_h, head_h,
    rows_out, kv_out, head_out,
    tok, q1, q2, tea, w_full, head_full, kv, probs, probs_b, hidden, grad_h, grad_o, normed_b,
    tok_t, norm_t, tok_t_all, norm_t_all, kvg_all, gl_all, grad_rows, pack, unpack,
    part, y_in, z_out, z_in, kv_sum, hpart, hy_in, hz_in, head_sum,
    send_sem, recv_sem, local_sem,
):
    g, f = lax.axis_index("dp"), lax.axis_index("fsdp")
    z, lo = g // 2, g % 2
    hi, x, c = f // 8, (f // 2) % 4, f % 2

    def at(z_, lo_, hi_, x_, c_):
        return (z_ * 2 + lo_, hi_ * 8 + x_ * 2 + c_)

    def xk(k):
        return (x + k) % 4

    def zk(k):
        return (z + k) % Z

    other = at(z, lo, hi, x, 1 - c)
    y_far = at(z, 1 - lo, 1 - hi, x, c)
    y_pair = at(z, 1 - lo, hi, x, c)
    y_two = at(z, lo, 1 - hi, x, c)

    loads = []
    for n, (src, dst) in enumerate(((tok_h, tok), (q1_h, q1), (q2_h, q2), (tea_h, tea))):
        load = pltpu.make_async_copy(src, dst, local_sem.at[n])
        load.start()
        loads.append(load)
    own_rows = rows_at(f * SHARD, SHARD)
    for n, (src, dst) in enumerate(((w_h, w_full), (head_h, head_full))):
        load = pltpu.make_async_copy(src, dst.at[own_rows], local_sem.at[4 + n])
        load.start()
        loads.append(load)

    peers = [other, y_far, y_two]
    for k in (1, 2, 3):
        peers += [at(z, lo, hi, xk(k), c), at(z, lo, hi, xk(k), 1 - c)]
    for k in range(16):
        if k:
            peers.append(((g + k) % 16, f))
    barrier = pltpu.get_barrier_semaphore()
    for peer in peers:
        pl.semaphore_signal(barrier, inc=1, device_id=peer, device_id_type=MESH)
    pl.semaphore_wait(barrier, len(peers))

    wires = Wires(send_sem, recv_sem, other)

    def shard(full, hi_, x_, c_):
        return full.at[rows_at((hi_ * 8 + x_ * 2 + c_) * SHARD, SHARD)]

    def half(full, hi_, x_, c_, lo_):
        return full.at[rows_at((hi_ * 8 + x_ * 2 + c_) * SHARD + lo_ * HALF, HALF)]

    order = (0, 1, 3, 2)

    def gather_x(source, full):
        own = full.at[own_rows]
        n_x = {k: wires.start(source, own, at(z, lo, hi, xk(k), c)) for k in (1, 3, 2)}
        return n_x

    def gather_far(own_loaded, full, n_x):
        n_far, n_core = {}, []
        own_loaded.wait()
        for k in order:
            if k:
                wires.arrived(n_x[k], shard(full, hi, xk(4 - k), c))
            src = half(full, hi, xk(4 - k), c, 1 - lo)
            n_far[k] = wires.start(src, src, y_far)
            src = shard(full, hi, xk(4 - k), c)
            n_core.append((wires.start(src, src, other), shard(full, hi, xk(4 - k), 1 - c)))
        return n_far, n_core

    def gather_pair(full, n_far, n_core):
        n_pair = {}
        for k in order:
            src = half(full, 1 - hi, xk(4 - k), c, lo)
            wires.arrived(n_far[k], src)
            n_pair[k] = wires.start(src, src, y_pair)
            n_core.append((wires.start(src, src, other), half(full, 1 - hi, xk(4 - k), 1 - c, lo)))
        return n_pair

    def gather_core(full, n_pair, n_core):
        for k in order:
            src = half(full, 1 - hi, xk(4 - k), c, 1 - lo)
            wires.arrived(n_pair[k], src)
            n_core.append((wires.start(src, src, other), half(full, 1 - hi, xk(4 - k), 1 - c, 1 - lo)))
        for n, landed in n_core:
            wires.arrived(n, landed)

    n_x = gather_x(w_h, w_full)
    loads[0].wait()

    def transpose_tokens(b, carry):
        tok_t[rows_at(b * D, D, D), :] = tok[:, lanes(b)].T
        return carry

    lax.fori_loop(0, HEADS, transpose_tokens, 0)

    n_far, n_core = gather_far(loads[4], w_full, n_x)

    lens = len_ref[:, 0, :].astype(F32)
    counts = cnt_ref[:, 0, :].astype(F32)
    len_row = len_ref[g].astype(F32)
    cnt_row = cnt_ref[g].astype(F32)

    def lane_sum(a):
        return jnp.sum(a, axis=1, keepdims=True)

    def row_sum(a):
        return jnp.sum(a, axis=0, keepdims=True)

    ends_col = lane_sum(jnp.where(iota((32, 32), 1) <= iota((32, 32), 0), len_row, 0.0))
    len_col = lane_sum(jnp.where(iota((32, 32), 1) == iota((32, 32), 0), len_row, 0.0))
    ends_row = row_sum(jnp.where(iota((32, 32), 0) <= iota((32, 32), 1), len_col, 0.0))
    seg_col = lane_sum(jnp.where(iota((ROWS, 32), 0).astype(F32) >= ends_row, 1.0, 0.0))
    seg_row = row_sum(jnp.where(iota((32, ROWS), 1).astype(F32) >= ends_col, 1.0, 0.0))
    visible = (seg_col == seg_row) & (iota((ROWS, ROWS), 0) <= iota((ROWS, ROWS), 1))
    bias = jnp.where(visible, 0.0, -1e30).astype(F32)

    start_col = lane_sum(jnp.where(iota((16, 16), 1) < iota((16, 16), 0), cnt_row, 0.0))
    stop_col = lane_sum(jnp.where(iota((16, 16), 1) <= iota((16, 16), 0), cnt_row, 0.0))
    k_row = iota((16, 32), 1).astype(F32)
    begin_col = lane_sum(jnp.where(k_row < start_col, len_row, 0.0))
    size_col = lane_sum(jnp.where(k_row < stop_col, len_row, 0.0)) - begin_col
    spread = jnp.where(iota((256, 16), 0) // 16 == iota((256, 16), 1), 1.0, 0.0)
    begin = lane_sum(jnp.where(spread > 0.0, row_sum(jnp.where(iota((16, 16), 0) == iota((16, 16), 1), begin_col, 0.0)), 0.0))
    size = lane_sum(jnp.where(spread > 0.0, row_sum(jnp.where(iota((16, 16), 0) == iota((16, 16), 1), size_col, 0.0)), 0.0))
    slot = (iota((256, ROWS), 0) % 16).astype(F32)
    row_id = iota((256, ROWS), 1).astype(F32)
    main = jnp.where((slot < 12.0) & (slot < size) & (row_id == begin + slot), 1.0, 0.0)
    pack_lhs = []
    for r in range(3):
        w = slot - (12.0 - 4.0 * r)
        rest = jnp.where((slot >= 12.0) & (w < size) & (row_id == begin + w), 1.0, 0.0)
        pack_lhs.append(jnp.concatenate([main, rest], axis=1).astype(BF16))

    start_in = lane_sum(jnp.where(iota((16, 16), 1) < g, counts, 0.0))
    stop_in = lane_sum(jnp.where(iota((16, 16), 1) <= g, counts, 0.0))
    size_in = lane_sum(jnp.where((k_row >= start_in) & (k_row < stop_in), lens, 0.0))
    group = iota((16, 256), 1) // 16
    size_row = row_sum(jnp.where(group == iota((16, 256), 0), size_in, 0.0))
    base_row = row_sum(jnp.where(iota((16, 256), 0) < group, size_in, 0.0))
    slot = (iota((ROWS, 256), 1) % 16).astype(F32)
    place = iota((ROWS, 256), 0).astype(F32)
    unpack_main = jnp.where((slot < 12.0) & (slot < size_row) & (place == base_row + slot), 1.0, 0.0).astype(BF16)
    unpack_rest = []
    for r in range(3):
        w = slot - (12.0 - 4.0 * r)
        unpack_rest.append(jnp.where((slot >= 12.0) & (w < size_row) & (place == base_row + w), 1.0, 0.0).astype(BF16))

    n_pair = gather_pair(w_full, n_far, n_core)
    n_hx = gather_x(head_h, head_full)
    gather_core(w_full, n_pair, n_core)

    def project(b, carry):
        cols = pl.ds(pl.multiple_of(b * 256, 256), 256)
        kv[:, cols] = dot(tok[...], w_full[:, cols]).astype(BF16)
        return carry

    lax.fori_loop(0, KV // 256, project, 0)

    p = x * 2 + c

    def exchange_t(mine, everyone):
        numbers = []
        for k in (0, 1, 3, 2):
            for flip in (0, 1):
                if k == 0 and flip == 0:
                    continue
                c_to = c if flip == 0 else 1 - c
                p_to = xk(k) * 2 + c_to
                p_from = xk(4 - k) * 2 + c_to
                for h_ in (0, 1):
                    src = mine.at[rows_at(h_ * 1280 + p_to * SHARD, SHARD), :]
                    dst = everyone.at[rows_at(h_ * SHARD, SHARD), lanes(p)]
                    n = wires.start(src, dst, at(z, lo, hi, xk(k), c_to))
                    numbers.append((n, everyone.at[rows_at(h_ * SHARD, SHARD), lanes(p_from)]))
        for h_ in (0, 1):
            everyone[rows_at(h_ * SHARD, SHARD), lanes(p)] = mine[rows_at(h_ * 1280 + p * SHARD, SHARD), :]
        return numbers

    n_tok = exchange_t(tok_t, tok_t_all)
    n_hfar, n_hcore = gather_far(loads[5], head_full, n_hx)
    loads[1].wait()
    loads[2].wait()

    def softmax_cols(scores):
        s = scores * (SCALE * LOG2E) + bias
        e = jnp.exp2(s - jnp.max(s, axis=0, keepdims=True))
        return e * (1.0 / jnp.sum(e, axis=0, keepdims=True))

    def attend(j, squares):
        keys = kv[:, lanes(j)]
        values = kv[:, lanes(KV_HEADS + j)]
        for i in range(PER_KEY):
            h = j * PER_KEY + i
            one = softmax_cols(dot_nt(keys, q1[:, lanes(h)]))
            two = softmax_cols(dot_nt(keys, q2[:, lanes(h)]))
            probs[2 * h] = one
            probs[2 * h + 1] = two
            both = (one + two).astype(BF16)
            probs_b[h] = both
            hid = tok[:, lanes(h)].astype(F32) + dot(both.T, values)
            hidden[:, lanes(h)] = hid
            squares = squares + hid * hid
        return squares

    squares = lax.fori_loop(0, 2, attend, jnp.zeros((ROWS, D), F32))
    n_hpair = gather_pair(head_full, n_hfar, n_hcore)
    squares = lax.fori_loop(2, 4, attend, squares)
    inverse = lax.rsqrt(jnp.sum(squares, axis=1, keepdims=True) * (1.0 / WIDTH) + EPS)

    def normalise(b, carry):
        n_b = (hidden[:, lanes(b)] * inverse).astype(BF16)
        normed_b[:, lanes(b)] = n_b
        norm_t[rows_at(b * D, D, D), :] = n_b.T
        return carry

    lax.fori_loop(0, HEADS, normalise, 0)
    gather_core(head_full, n_hpair, n_hcore)
    loads[3].wait()

    def softmax_rows(a):
        e = jnp.exp(a - jnp.max(a, axis=1, keepdims=True))
        return e / jnp.sum(e, axis=1, keepdims=True)

    student = softmax_rows(dot(normed_b[...], head_full[...]))
    grad_logits = (student - softmax_rows(tea[...].astype(F32))).astype(BF16)
    mine = rows_at(p * ROWS, ROWS, ROWS)
    gl_all[mine, :] = grad_logits

    def ring_x(everyone, cols):
        src = everyone.at[mine, cols]
        out = {k: wires.start(src, src, at(z, lo, hi, xk(k), c)) for k in (1, 3, 2)}
        return out, [(wires.start(src, src, other), everyone.at[rows_at((x * 2 + 1 - c) * ROWS, ROWS, ROWS), cols])]

    def relay_x(everyone, cols, out, core):
        for k in (1, 3, 2):
            src = everyone.at[rows_at((xk(4 - k) * 2 + c) * ROWS, ROWS, ROWS), cols]
            wires.arrived(out[k], src)
            core.append((wires.start(src, src, other), everyone.at[rows_at((xk(4 - k) * 2 + 1 - c) * ROWS, ROWS, ROWS), cols]))

    def wait_core(core):
        for n, landed in core:
            wires.arrived(n, landed)

    gl_cols = pl.ds(0, VOCAB)
    n_gl, n_gl_core = ring_x(gl_all, gl_cols)
    n_norm = exchange_t(norm_t, norm_t_all)

    def back_head(b, dots):
        cols = pl.ds(pl.multiple_of(b * 512, 512), 512)
        gn = dot_nt(grad_logits, head_full[cols, :])
        grad_h[:, cols] = gn
        prod = gn * (hidden[:, cols] * inverse)
        for q in range(4):
            dots = dots + prod[:, q * D:(q + 1) * D]
        return dots

    dots = lax.fori_loop(0, WIDTH // 512, back_head, jnp.zeros((ROWS, D), F32))
    mean = jnp.sum(dots, axis=1, keepdims=True) * (1.0 / WIDTH)

    def back_norm(b, carry):
        cols = pl.ds(pl.multiple_of(b * 512, 512), 512)
        gh = inverse * (grad_h[:, cols] - (hidden[:, cols] * inverse) * mean)
        grad_h[:, cols] = gh
        grad_o[:, cols] = gh.astype(BF16)
        return carry

    lax.fori_loop(0, WIDTH // 512, back_norm, 0)

    def attend_back(j, carry):
        values = kv[:, lanes(KV_HEADS + j)]
        gk = jnp.zeros((ROWS, D), F32)
        gv = jnp.zeros((ROWS, D), F32)
        for i in range(PER_KEY):
            h = j * PER_KEY + i
            go = grad_o[:, lanes(h)]
            gp = dot_nt(values, go)
            gv = gv + dot(probs_b[h], go)
            for layer, queries in enumerate((q1, q2)):
                pr = probs[2 * h + layer]
                along = jnp.sum(pr * gp, axis=0, keepdims=True)
                gs = (pr * (gp - along) * SCALE).astype(BF16)
                gk = gk + dot(gs, queries[:, lanes(h)])
        kvg_all[mine, lanes(j)] = gk.astype(BF16)
        kvg_all[mine, lanes(KV_HEADS + j)] = gv.astype(BF16)
        return carry

    lax.fori_loop(0, 2, attend_back, 0)
    relay_x(gl_all, gl_cols, n_gl, n_gl_core)
    lax.fori_loop(2, 4, attend_back, 0)

    kvg_cols = pl.ds(0, KV)
    n_kvg, n_kvg_core = ring_x(kvg_all, kvg_cols)

    def back_rows(b, carry):
        cols = pl.ds(pl.multiple_of(b * 512, 512), 512)
        back = dot_nt(kvg_all[mine, :], w_full[cols, :])
        grad_rows[:, cols] = (grad_h[:, cols] + back).astype(BF16)
        return carry

    lax.fori_loop(0, WIDTH // 512, back_rows, 0)
    for e in range(5):
        rest = grad_rows[:, (15 + e) * D:(16 + e) * D]
        for r in range(3):
            b = 3 * e + r
            both = jnp.concatenate([grad_rows[:, b * D:(b + 1) * D], rest], axis=0)
            pack[:, b * D:(b + 1) * D] = dot(pack_lhs[r], both).astype(BF16)
    n_rows = []
    for k in range(1, 16):
        n = wires.start(pack.at[rows_at((g + k) % 16 * 16, 16)], unpack.at[rows_at(g * 16, 16)], ((g + k) % 16, f))
        n_rows.append((n, unpack.at[rows_at((g + 16 - k) % 16 * 16, 16)]))
    unpack[rows_at(g * 16, 16), :] = pack[rows_at(g * 16, 16), :]

    def quarter(ref, hi_, lo_):
        return ref.at[rows_at(hi_ * SHARD + lo_ * HALF, HALF), :]

    def scatter_y(ref, landing):
        out = []
        for n, (to, hi_, lo_) in enumerate(((y_far, 1 - hi, 1 - lo), (y_pair, hi, 1 - lo), (y_two, 1 - hi, lo))):
            out.append((wires.start(quarter(ref, hi_, lo_), landing.at[n], to), landing.at[n]))
        return out

    own_quarter = rows_at(hi * SHARD + lo * HALF, HALF)
    for n, landed in n_norm:
        wires.arrived(n, landed)
    wait_core(n_gl_core)
    hpart[...] = dot(norm_t_all[...], gl_all[...]).astype(BF16)
    n_hy = scatter_y(hpart, hy_in)

    relay_x(kvg_all, kvg_cols, n_kvg, n_kvg_core)
    for n, landed in n_tok:
        wires.arrived(n, landed)
    wait_core(n_kvg_core)

    def product(b, carry):
        cols = pl.ds(pl.multiple_of(b * 256, 256), 256)
        part[:, cols] = dot(tok_t_all[...], kvg_all[:, cols]).astype(BF16)
        return carry

    lax.fori_loop(0, KV // 256, product, 0)
    n_y = scatter_y(part, y_in)

    for n, landed in n_hy:
        wires.arrived(n, landed)
    total = hpart[own_quarter, :].astype(F32)
    for n in range(3):
        total = total + hy_in[n].astype(F32)
    hz_in[z] = total.astype(BF16)
    n_hz = []
    for k in (1, 7, 2, 6, 3, 5, 4):
        n = wires.start(hz_in.at[z], hz_in.at[z], at(zk(k), lo, hi, x, c))
        n_hz.append((n, hz_in.at[zk(Z - k)]))

    for n, landed in n_y:
        wires.arrived(n, landed)

    def add_y(b, carry):
        total = part[own_quarter, lanes(b)].astype(F32)
        for n in range(3):
            total = total + y_in[n, :, lanes(b)].astype(F32)
        z_out[b] = total.astype(BF16)
        return carry

    lax.fori_loop(0, Z, add_y, 0)
    n_z = []
    for k in (4, 3, 5, 2, 6, 1, 7):
        n = wires.start(z_out.at[zk(k)], z_in.at[z], at(zk(k), lo, hi, x, c))
        n_z.append((n, z_in.at[zk(Z - k)]))
    z_in[z] = z_out[z]

    for n, landed in n_hz:
        wires.arrived(n, landed)
    total = hz_in[0].astype(F32)
    for n in range(1, Z):
        total = total + hz_in[n].astype(F32)
    head_sum[lo] = total.astype(BF16)
    n_hp = wires.start(head_sum.at[lo], head_sum.at[lo], y_pair)

    for n, landed in n_z:
        wires.arrived(n, landed)
    total = z_in[0].astype(F32)
    for n in range(1, Z):
        total = total + z_in[n].astype(F32)
    kv_sum[lo, z] = total.astype(BF16)
    n_zg, n_pair = {}, []
    for k in (4, 3, 5, 2, 6, 1, 7):
        n_zg[k] = wires.start(kv_sum.at[lo, z], kv_sum.at[lo, z], at(zk(k), lo, hi, x, c))
    n_pair.append((wires.start(kv_sum.at[lo, z], kv_sum.at[lo, z], y_pair), kv_sum.at[1 - lo, z]))

    for n, landed in n_rows:
        wires.arrived(n, landed)
    rows_out[:, :15 * D] = dot(unpack_main, unpack[...]).astype(BF16)
    for e in range(5):
        acc = dot(unpack_rest[0], unpack[:, 3 * e * D:(3 * e + 1) * D])
        for r in (1, 2):
            acc = acc + dot(unpack_rest[r], unpack[:, (3 * e + r) * D:(3 * e + r + 1) * D])
        rows_out[:, (15 + e) * D:(16 + e) * D] = acc.astype(BF16)

    for k in (1, 7, 2, 6, 3, 5, 4):
        src = kv_sum.at[lo, zk(Z - k)]
        wires.arrived(n_zg[k], src)
        n_pair.append((wires.start(src, src, y_pair), kv_sum.at[1 - lo, zk(Z - k)]))
    wires.arrived(n_hp, head_sum.at[1 - lo])
    for l in range(2):
        head_out[l * HALF:(l + 1) * HALF, :] = head_sum[l].astype(F32)
    for n, landed in n_pair:
        wires.arrived(n, landed)
    for l in range(2):
        for b in range(Z):
            kv_out[l * HALF:(l + 1) * HALF, b * D:(b + 1) * D] = kv_sum[l, b].astype(F32)
    wires.drain()


def on_device(tokens_in, queries_first, queries_second, teacher_logits, rollout_lengths, send_counts, key_value_weight, head_slice):
    big = pl.BlockSpec(memory_space=pl.ANY)
    small = pl.BlockSpec(memory_space=pltpu.VMEM)

    def buf(*shape, dtype=BF16):
        return pltpu.VMEM(shape, dtype)

    return pl.pallas_call(
        kernel,
        out_shape=(
            jax.ShapeDtypeStruct((ROWS, WIDTH), BF16),
            jax.ShapeDtypeStruct((SHARD, KV), F32),
            jax.ShapeDtypeStruct((SHARD, VOCAB), F32),
        ),
        in_specs=[big, big, big, big, small, small, big, big],
        out_specs=(small, small, small),
        scratch_shapes=[
            buf(ROWS, WIDTH), buf(ROWS, WIDTH), buf(ROWS, WIDTH), buf(ROWS, VOCAB),
            buf(WIDTH, KV), buf(WIDTH, VOCAB), buf(ROWS, KV),
            buf(2 * HEADS, ROWS, D, dtype=F32), buf(HEADS, ROWS, D),
            buf(ROWS, WIDTH, dtype=F32), buf(ROWS, WIDTH, dtype=F32), buf(ROWS, WIDTH), buf(ROWS, WIDTH),
            buf(WIDTH, ROWS), buf(WIDTH, ROWS), buf(2 * SHARD, 8 * ROWS), buf(2 * SHARD, 8 * ROWS),
            buf(8 * ROWS, KV), buf(8 * ROWS, VOCAB), buf(ROWS, WIDTH),
            buf(256, 15 * D), buf(256, 15 * D),
            buf(2 * SHARD, KV), buf(3, HALF, KV), buf(Z, HALF, D), buf(Z, HALF, D), buf(2, Z, HALF, D),
            buf(2 * SHARD, VOCAB), buf(3, HALF, VOCAB), buf(Z, HALF, VOCAB), buf(2, HALF, VOCAB),
            pltpu.SemaphoreType.DMA((COPIES,)), pltpu.SemaphoreType.DMA((COPIES,)), pltpu.SemaphoreType.DMA((6,)),
        ],
        compiler_params=pltpu.CompilerParams(collective_id=0, has_side_effects=True, vmem_limit_bytes=48 * 2**20),
        name="pair_backward",
    )(tokens_in, queries_first, queries_second, teacher_logits, rollout_lengths, send_counts, key_value_weight, head_slice)


def solution(mesh):
    in_specs = (
        P(("dp", "fsdp"), None),
        P(("dp", "fsdp"), None),
        P(("dp", "fsdp"), None),
        P(("dp", "fsdp"), None),
        P(None, "fsdp", None),
        P(None, "fsdp", None),
        P("fsdp", None),
        P("fsdp", None),
    )
    out_specs = (P(("dp", "fsdp"), None), P("fsdp", None), P("fsdp", None))
    return jax.shard_map(on_device, mesh=mesh, in_specs=in_specs, out_specs=out_specs, check_vma=False)
```

time: 498 us -> 124 us (0.25)
  the two profiles are of different devices: /device:TPU:2 before, /device:TPU:1 now
where the time goes in v2:
time: 124 us
  Pallas kernels  114 us (92%)
  local copies, waits for them, and re-layouts  9.68 us (8%)
    pallas_call x1, Pallas kernels, on_device(): pl.pallas_call(kernel, out_shape=(jax.ShapeDtypeStruct((ROWS, WIDTH), BF1...  114 us
    unnamed x19, local copies, waits for them, and re-layouts  9.68 us

profile of v2, /device:TPU:1, one launch (start us, length us, event | category | flops | bytes accessed | tf_op | source)
XLA Modules:
  0.0 124.0 jit_solution(13769930176932740489)
XLA Ops:
  0.6 0.0 copy-start
  0.6 1.1 copy-done
  1.7 0.0 copy-start.1
  1.7 1.1 copy-done.1
  2.8 0.0 copy-start.2
  2.8 1.1 copy-done.2
  3.9 0.0 copy-start.3
  3.9 1.0 copy-done.3
  4.9 0.0 copy-start.4
  4.9 0.9 copy-done.4
  5.8 0.0 copy-start.5
  5.8 0.8 copy-done.5
  6.6 0.0 copy-start.6
  6.6 0.7 copy-done.6
  7.3 0.0 copy-start.7
  7.3 0.7 copy-done.7
  8.0 113.6 %pair_backward.1 = (bf16[128,2560]{1,0:T(8,128)(2,1)S(1)}, f32[160,1024]{1,0:T(8,128)S(1)}, f32[160,256]{1,0:T(8,128)S(1)}) custom-call(bf16[128,2560]{1,0:T(8,128)(2,1)S(1)} %copy-done, bf16[128,2560]{1,0:T(8,128)(2,1)S(1)} %copy-done.1, bf16[128,2560]{1,0:T(8,128)(2,1)S(1)} %copy-done.2, bf16[128,256]{1,0:T(8,128)(2,1)S(1)} %copy-done.5, ...), custom_call_target="tpu_custom_call" | custom-call | tf_op jit(solution)/shard_map/pair_backward/pallas_call | solution.py:503
  121.6 0.8 copy.14
  122.5 0.8 copy.15
  123.3 0.7 copy.16
Async XLA Ops:
  0.6 1.1 copy-start
  1.7 1.1 copy-start.1
  2.8 1.1 copy-start.2
  3.9 1.0 copy-start.3
  4.9 0.9 copy-start.4
  5.8 0.8 copy-start.5
  6.6 0.7 copy-start.6
  7.3 0.7 copy-start.7

commit v3 on v2

--- a/solution.py
+++ b/solution.py
@@ -24,7 +24,7 @@
 MESH = pl.DeviceIdType.MESH
 F32 = jnp.float32
 BF16 = jnp.bfloat16
-COPIES = 160
+COPIES = 200
 
 
 def iota(shape, dim):
@@ -79,8 +79,8 @@
     tok_h, q1_h, q2_h, tea_h, len_ref, cnt_ref, w_h, head_h,
     rows_out, kv_out, head_out,
     tok, q1, q2, tea, w_full, head_full, kv, probs, probs_b, hidden, grad_h, grad_o, normed_b,
-    tok_t, norm_t, tok_t_all, norm_t_all, kvg_all, gl_all, grad_rows, pack, unpack,
-    part, y_in, z_out, z_in, kv_sum, hpart, hy_in, hz_in, head_sum,
+    tok_tx, tok_ty, norm_ty, tok_x_all, tok_y_all, norm_y_all, keys_all, vals_all, grad_rows, pack, unpack,
+    part_x, part_y, y_in, x_in, z_out, z_in, kv_sum,
     send_sem, recv_sem, local_sem,
 ):
     g, f = lax.axis_index("dp"), lax.axis_index("fsdp")
@@ -95,6 +95,10 @@
 
     def zk(k):
         return (z + k) % Z
+
+    def yk(k):
+        y_ = (hi * 2 + lo + k) % 4
+        return y_ // 2, y_ % 2
 
     other = at(z, lo, hi, x, 1 - c)
     y_far = at(z, 1 - lo, 1 - hi, x, c)
@@ -112,7 +116,7 @@
         load.start()
         loads.append(load)
 
-    peers = [other, y_far, y_two]
+    peers = [other, y_far, y_two, at(z, 1 - lo, 1 - hi, x, 1 - c), at(z, 1 - lo, hi, x, 1 - c), at(z, lo, 1 - hi, x, 1 - c)]
     for k in (1, 2, 3):
         peers += [at(z, lo, hi, xk(k), c), at(z, lo, hi, xk(k), 1 - c)]
     for k in range(16):
@@ -164,19 +168,96 @@
             src = half(full, 1 - hi, xk(4 - k), c, 1 - lo)
             wires.arrived(n_pair[k], src)
             n_core.append((wires.start(src, src, other), half(full, 1 - hi, xk(4 - k), 1 - c, 1 - lo)))
-        for n, landed in n_core:
-            wires.arrived(n, landed)
-
-    n_x = gather_x(w_h, w_full)
+
+    kept = pl.ds(pl.multiple_of(z % 2 * (KV // 2), KV // 2), KV // 2)
+    given = pl.ds(pl.multiple_of((1 - z % 2) * (KV // 2), KV // 2), KV // 2)
+
+    def block(hi_, x_, c_, cols, half_=None):
+        start = (hi_ * 8 + x_ * 2 + c_) * SHARD
+        if half_ is None:
+            return w_full.at[rows_at(start, SHARD), cols]
+        return w_full.at[rows_at(start + half_ * HALF, HALF), cols]
+
+    w_core, w_z = [], []
+
+    def to_core(hi_, x_, cols, half_=None):
+        src = block(hi_, x_, c, cols, half_)
+        w_core.append((wires.start(src, src, other), block(hi_, x_, 1 - c, cols, half_)))
+
+    def to_z(hi_, x_, half_):
+        src = block(hi_, x_, c, kept, half_)
+        n = wires.start(src, src, at((z + 1 - 2 * half_ + Z) % Z, lo, hi, x, c))
+        w_z.append((n, hi_, x_, half_))
+
+    def to_far(x_):
+        src = block(hi, x_, c, kept, 1 - lo)
+        return wires.start(src, src, y_far)
+
+    loads[4].wait()
+    n_x, n_far, n_pair = {}, {}, {}
+    n_far[0] = to_far(x)
+    for k, half_ in ((1, 1 - lo), (3, 1 - lo), (1, lo), (3, lo), (2, 1 - lo), (2, lo)):
+        src = block(hi, x, c, kept, half_)
+        n_x.setdefault(k, []).append(wires.start(src, src, at(z, lo, hi, xk(k), c)))
+    to_core(hi, x, pl.ds(0, KV))
     loads[0].wait()
 
-    def transpose_tokens(b, carry):
-        tok_t[rows_at(b * D, D, D), :] = tok[:, lanes(b)].T
+    def turn_rows(ref, m):
+        blocks = [ref[:, lanes(5 * m + i)].T for i in range(5)]
+        return jnp.concatenate(blocks, axis=0)
+
+    def units(turned, m):
+        for i in range(8):
+            yield m // 2, m % 2 * 2 + i // 4, i // 2 % 2, i % 2, turned[i * HALF:(i + 1) * HALF, :]
+
+    def y_order(h_, x_, c_, half_):
+        return rows_at(((h_ * 2 + half_) * 2 + c_) * 2 * SHARD + x_ * HALF, HALF)
+
+    def transpose_tokens(m, carry):
+        for h_, x_, c_, half_, unit in units(turn_rows(tok, m), m):
+            tok_tx[rows_at((x_ * 2 + c_) * 2 * SHARD + h_ * SHARD + half_ * HALF, HALF), :] = unit
+            tok_ty[y_order(h_, x_, c_, half_), :] = unit
         return carry
 
-    lax.fori_loop(0, HEADS, transpose_tokens, 0)
-
-    n_far, n_core = gather_far(loads[4], w_full, n_x)
+    lax.fori_loop(0, 4, transpose_tokens, 0)
+
+    def got_x(k, turn):
+        x_ = xk(4 - k)
+        half_ = lo if turn else 1 - lo
+        wires.arrived(n_x[k][turn], block(hi, x_, c, kept, half_))
+        to_z(hi, x_, half_)
+        if not turn:
+            n_far[k] = to_far(x_)
+        to_core(hi, x_, kept, half_)
+
+    def got_far(k):
+        x_ = xk(4 - k)
+        src = block(1 - hi, x_, c, kept, lo)
+        wires.arrived(n_far[k], src)
+        n_pair[k] = wires.start(src, src, y_pair)
+        to_z(1 - hi, x_, lo)
+        to_core(1 - hi, x_, kept, lo)
+
+    def got_pair(k):
+        x_ = xk(4 - k)
+        wires.arrived(n_pair[k], block(1 - hi, x_, c, kept, 1 - lo))
+        to_z(1 - hi, x_, 1 - lo)
+        to_core(1 - hi, x_, kept, 1 - lo)
+
+    got_far(0)
+    got_x(1, 0)
+    got_x(3, 0)
+    got_x(1, 1)
+    got_x(3, 1)
+    got_pair(0)
+    n_hx = gather_x(head_h, head_full)
+    got_far(1)
+    got_far(3)
+    got_x(2, 0)
+    got_x(2, 1)
+    got_pair(1)
+    got_pair(3)
+    got_far(2)
 
     lens = len_ref[:, 0, :].astype(F32)
     counts = cnt_ref[:, 0, :].astype(F32)
@@ -228,9 +309,16 @@
         w = slot - (12.0 - 4.0 * r)
         unpack_rest.append(jnp.where((slot >= 12.0) & (w < size_row) & (place == base_row + w), 1.0, 0.0).astype(BF16))
 
-    n_pair = gather_pair(w_full, n_far, n_core)
-    n_hx = gather_x(head_h, head_full)
-    gather_core(w_full, n_pair, n_core)
+    got_pair(2)
+    n_hfar, n_hcore = gather_far(loads[5], head_full, n_hx)
+    n_hpair = None
+    for i, (n, hi_, x_, half_) in enumerate(w_z):
+        if i == 10:
+            n_hpair = gather_pair(head_full, n_hfar, n_hcore)
+        wires.arrived(n, block(hi_, x_, c, given, half_))
+        to_core(hi_, x_, given, half_)
+    for n, landed in w_core:
+        wires.arrived(n, landed)
 
     def project(b, carry):
         cols = pl.ds(pl.multiple_of(b * 256, 256), 256)
@@ -239,28 +327,25 @@
 
     lax.fori_loop(0, KV // 256, project, 0)
 
-    p = x * 2 + c
-
-    def exchange_t(mine, everyone):
+    def on_ring(along_x, k, c_):
+        if along_x:
+            return at(z, lo, hi, xk(k), c_), xk(k) * 2 + c_
+        hi_, lo_ = yk(k)
+        return at(z, lo_, hi_, x, c_), (hi_ * 2 + lo_) * 2 + c_
+
+    def exchange_t(mine, everyone, along_x):
         numbers = []
-        for k in (0, 1, 3, 2):
-            for flip in (0, 1):
-                if k == 0 and flip == 0:
-                    continue
-                c_to = c if flip == 0 else 1 - c
-                p_to = xk(k) * 2 + c_to
-                p_from = xk(4 - k) * 2 + c_to
-                for h_ in (0, 1):
-                    src = mine.at[rows_at(h_ * 1280 + p_to * SHARD, SHARD), :]
-                    dst = everyone.at[rows_at(h_ * SHARD, SHARD), lanes(p)]
-                    n = wires.start(src, dst, at(z, lo, hi, xk(k), c_to))
-                    numbers.append((n, everyone.at[rows_at(h_ * SHARD, SHARD), lanes(p_from)]))
-        for h_ in (0, 1):
-            everyone[rows_at(h_ * SHARD, SHARD), lanes(p)] = mine[rows_at(h_ * 1280 + p * SHARD, SHARD), :]
+        spot = on_ring(along_x, 0, c)[1]
+        for k, c_ in ((1, c), (3, c), (1, 1 - c), (3, 1 - c), (2, c), (2, 1 - c), (0, 1 - c)):
+            to, p_to = on_ring(along_x, k, c_)
+            p_from = on_ring(along_x, 4 - k, c_)[1]
+            n = wires.start(mine.at[rows_at(p_to * 2 * SHARD, 2 * SHARD), :], everyone.at[:, lanes(spot)], to)
+            numbers.append((n, everyone.at[:, lanes(p_from)]))
+        everyone[:, lanes(spot)] = mine[rows_at(spot * 2 * SHARD, 2 * SHARD), :]
         return numbers
 
-    n_tok = exchange_t(tok_t, tok_t_all)
-    n_hfar, n_hcore = gather_far(loads[5], head_full, n_hx)
+    n_tx = exchange_t(tok_tx, tok_x_all, True)
+    n_ty = exchange_t(tok_ty, tok_y_all, False)
     loads[1].wait()
     loads[2].wait()
 
@@ -286,18 +371,21 @@
         return squares
 
     squares = lax.fori_loop(0, 2, attend, jnp.zeros((ROWS, D), F32))
-    n_hpair = gather_pair(head_full, n_hfar, n_hcore)
+    gather_core(head_full, n_hpair, n_hcore)
     squares = lax.fori_loop(2, 4, attend, squares)
     inverse = lax.rsqrt(jnp.sum(squares, axis=1, keepdims=True) * (1.0 / WIDTH) + EPS)
 
-    def normalise(b, carry):
-        n_b = (hidden[:, lanes(b)] * inverse).astype(BF16)
-        normed_b[:, lanes(b)] = n_b
-        norm_t[rows_at(b * D, D, D), :] = n_b.T
+    def normalise(m, carry):
+        cols = pl.ds(pl.multiple_of(m * 640, 640), 640)
+        normed_b[:, cols] = (hidden[:, cols] * inverse).astype(BF16)
+        for h_, x_, c_, half_, unit in units(turn_rows(normed_b, m), m):
+            norm_ty[y_order(h_, x_, c_, half_), :] = unit
         return carry
 
-    lax.fori_loop(0, HEADS, normalise, 0)
-    gather_core(head_full, n_hpair, n_hcore)
+    lax.fori_loop(0, 4, normalise, 0)
+    n_norm = exchange_t(norm_ty, norm_y_all, False)
+    for n, landed in n_hcore:
+        wires.arrived(n, landed)
     loads[3].wait()
 
     def softmax_rows(a):
@@ -306,27 +394,29 @@
 
     student = softmax_rows(dot(normed_b[...], head_full[...]))
     grad_logits = (student - softmax_rows(tea[...].astype(F32))).astype(BF16)
-    mine = rows_at(p * ROWS, ROWS, ROWS)
-    gl_all[mine, :] = grad_logits
-
-    def ring_x(everyone, cols):
-        src = everyone.at[mine, cols]
-        out = {k: wires.start(src, src, at(z, lo, hi, xk(k), c)) for k in (1, 3, 2)}
-        return out, [(wires.start(src, src, other), everyone.at[rows_at((x * 2 + 1 - c) * ROWS, ROWS, ROWS), cols])]
-
-    def relay_x(everyone, cols, out, core):
+    mine_x = rows_at(on_ring(True, 0, c)[1] * ROWS, ROWS, ROWS)
+    mine_y = rows_at(on_ring(False, 0, c)[1] * ROWS, ROWS, ROWS)
+    gl_cols = pl.ds(KV // 2, VOCAB)
+    vals_all[mine_y, gl_cols] = grad_logits
+
+    def ring_send(everyone, cols, along_x):
+        src = everyone.at[rows_at(on_ring(along_x, 0, c)[1] * ROWS, ROWS, ROWS), cols]
+        out = {k: wires.start(src, src, on_ring(along_x, k, c)[0]) for k in (1, 3, 2)}
+        landed = everyone.at[rows_at(on_ring(along_x, 0, 1 - c)[1] * ROWS, ROWS, ROWS), cols]
+        return out, [(wires.start(src, src, other), landed)]
+
+    def ring_relay(everyone, cols, along_x, out, core):
         for k in (1, 3, 2):
-            src = everyone.at[rows_at((xk(4 - k) * 2 + c) * ROWS, ROWS, ROWS), cols]
+            src = everyone.at[rows_at(on_ring(along_x, 4 - k, c)[1] * ROWS, ROWS, ROWS), cols]
             wires.arrived(out[k], src)
-            core.append((wires.start(src, src, other), everyone.at[rows_at((xk(4 - k) * 2 + 1 - c) * ROWS, ROWS, ROWS), cols]))
-
-    def wait_core(core):
-        for n, landed in core:
+            landed = everyone.at[rows_at(on_ring(along_x, 4 - k, 1 - c)[1] * ROWS, ROWS, ROWS), cols]
+            core.append((wires.start(src, src, other), landed))
+
+    def wait_all(numbers):
+        for n, landed in numbers:
             wires.arrived(n, landed)
 
-    gl_cols = pl.ds(0, VOCAB)
-    n_gl, n_gl_core = ring_x(gl_all, gl_cols)
-    n_norm = exchange_t(norm_t, norm_t_all)
+    n_gl = ring_send(vals_all, gl_cols, False)
 
     def back_head(b, dots):
         cols = pl.ds(pl.multiple_of(b * 512, 512), 512)
@@ -363,20 +453,19 @@
                 along = jnp.sum(pr * gp, axis=0, keepdims=True)
                 gs = (pr * (gp - along) * SCALE).astype(BF16)
                 gk = gk + dot(gs, queries[:, lanes(h)])
-        kvg_all[mine, lanes(j)] = gk.astype(BF16)
-        kvg_all[mine, lanes(KV_HEADS + j)] = gv.astype(BF16)
+        keys_all[mine_x, lanes(j)] = gk.astype(BF16)
+        vals_all[mine_y, lanes(j)] = gv.astype(BF16)
         return carry
 
-    lax.fori_loop(0, 2, attend_back, 0)
-    relay_x(gl_all, gl_cols, n_gl, n_gl_core)
-    lax.fori_loop(2, 4, attend_back, 0)
-
-    kvg_cols = pl.ds(0, KV)
-    n_kvg, n_kvg_core = ring_x(kvg_all, kvg_cols)
+    lax.fori_loop(0, KV_HEADS, attend_back, 0)
+
+    kv_cols = pl.ds(0, KV // 2)
+    n_keys = ring_send(keys_all, kv_cols, True)
+    n_vals = ring_send(vals_all, kv_cols, False)
 
     def back_rows(b, carry):
         cols = pl.ds(pl.multiple_of(b * 512, 512), 512)
-        back = dot_nt(kvg_all[mine, :], w_full[cols, :])
+        back = dot_nt(keys_all[mine_x, :], w_full[cols, :KV // 2]) + dot_nt(vals_all[mine_y, kv_cols], w_full[cols, KV // 2:])
         grad_rows[:, cols] = (grad_h[:, cols] + back).astype(BF16)
         return carry
 
@@ -388,75 +477,60 @@
             both = jnp.concatenate([grad_rows[:, b * D:(b + 1) * D], rest], axis=0)
             pack[:, b * D:(b + 1) * D] = dot(pack_lhs[r], both).astype(BF16)
     n_rows = []
-    for k in range(1, 16):
+    for k in (8, 7, 9, 6, 10, 5, 11, 4, 12, 3, 13, 2, 14, 1, 15):
         n = wires.start(pack.at[rows_at((g + k) % 16 * 16, 16)], unpack.at[rows_at(g * 16, 16)], ((g + k) % 16, f))
         n_rows.append((n, unpack.at[rows_at((g + 16 - k) % 16 * 16, 16)]))
     unpack[rows_at(g * 16, 16), :] = pack[rows_at(g * 16, 16), :]
 
-    def quarter(ref, hi_, lo_):
-        return ref.at[rows_at(hi_ * SHARD + lo_ * HALF, HALF), :]
-
-    def scatter_y(ref, landing):
-        out = []
-        for n, (to, hi_, lo_) in enumerate(((y_far, 1 - hi, 1 - lo), (y_pair, hi, 1 - lo), (y_two, 1 - hi, lo))):
-            out.append((wires.start(quarter(ref, hi_, lo_), landing.at[n], to), landing.at[n]))
-        return out
-
-    own_quarter = rows_at(hi * SHARD + lo * HALF, HALF)
-    for n, landed in n_norm:
-        wires.arrived(n, landed)
-    wait_core(n_gl_core)
-    hpart[...] = dot(norm_t_all[...], gl_all[...]).astype(BF16)
-    n_hy = scatter_y(hpart, hy_in)
-
-    relay_x(kvg_all, kvg_cols, n_kvg, n_kvg_core)
-    for n, landed in n_tok:
-        wires.arrived(n, landed)
-    wait_core(n_kvg_core)
-
-    def product(b, carry):
-        cols = pl.ds(pl.multiple_of(b * 256, 256), 256)
-        part[:, cols] = dot(tok_t_all[...], kvg_all[:, cols]).astype(BF16)
+    ring_relay(keys_all, kv_cols, True, *n_keys)
+    ring_relay(vals_all, gl_cols, False, *n_gl)
+    wait_all(n_tx)
+    wait_all(n_keys[1])
+    part_x[...] = dot(tok_x_all[...], keys_all[...]).astype(BF16)
+    n_y = []
+    for k in (1, 3, 2):
+        hi_, lo_ = yk(k)
+        n = wires.start(part_x.at[rows_at(hi_ * SHARD + lo_ * HALF, HALF), :], y_in.at[k - 1], on_ring(False, k, c)[0])
+        n_y.append((n, y_in.at[k - 1]))
+
+    ring_relay(vals_all, kv_cols, False, *n_vals)
+    wait_all(n_ty)
+    wait_all(n_norm)
+    wait_all(n_gl[1])
+    wait_all(n_vals[1])
+    part_y[:, kv_cols] = dot(tok_y_all[...], vals_all[:, kv_cols]).astype(BF16)
+    part_y[:, gl_cols] = dot(norm_y_all[...], vals_all[:, gl_cols]).astype(BF16)
+    for k in (1, 3, 2):
+        n = wires.start(part_y.at[rows_at(xk(k) * HALF, HALF), :], x_in.at[k - 1], on_ring(True, k, c)[0])
+        n_y.append((n, x_in.at[k - 1]))
+    own_x = rows_at(hi * SHARD + lo * HALF, HALF)
+    own_y = rows_at(x * HALF, HALF)
+
+    wait_all(n_y)
+
+    def add(own, parts, cols):
+        total = own.astype(F32)
+        for n in range(3):
+            total = total + parts[n, :, cols].astype(F32)
+        return total.astype(BF16)
+
+    def add_ring(b, carry):
+        z_out[b, :HALF, :] = add(part_x[own_x, lanes(b)], y_in, lanes(b))
+        z_out[b + 4, :HALF, :] = add(part_y[own_y, lanes(b)], x_in, lanes(b))
         return carry
 
-    lax.fori_loop(0, KV // 256, product, 0)
-    n_y = scatter_y(part, y_in)
-
-    for n, landed in n_hy:
-        wires.arrived(n, landed)
-    total = hpart[own_quarter, :].astype(F32)
-    for n in range(3):
-        total = total + hy_in[n].astype(F32)
-    hz_in[z] = total.astype(BF16)
-    n_hz = []
-    for k in (1, 7, 2, 6, 3, 5, 4):
-        n = wires.start(hz_in.at[z], hz_in.at[z], at(zk(k), lo, hi, x, c))
-        n_hz.append((n, hz_in.at[zk(Z - k)]))
-
-    for n, landed in n_y:
-        wires.arrived(n, landed)
-
-    def add_y(b, carry):
-        total = part[own_quarter, lanes(b)].astype(F32)
-        for n in range(3):
-            total = total + y_in[n, :, lanes(b)].astype(F32)
-        z_out[b] = total.astype(BF16)
-        return carry
-
-    lax.fori_loop(0, Z, add_y, 0)
+    lax.fori_loop(0, 4, add_ring, 0)
+    for v in range(2):
+        cols = slice(KV // 2 + v * D, KV // 2 + (v + 1) * D)
+        total = add(part_y[own_y, cols], x_in, cols)
+        for b in range(Z):
+            rows = total[b * 16:(b + 1) * 16] if b < 5 else jnp.zeros((16, D), BF16)
+            z_out[b, HALF + v * 16:HALF + (v + 1) * 16, :] = rows
     n_z = []
     for k in (4, 3, 5, 2, 6, 1, 7):
         n = wires.start(z_out.at[zk(k)], z_in.at[z], at(zk(k), lo, hi, x, c))
         n_z.append((n, z_in.at[zk(Z - k)]))
     z_in[z] = z_out[z]
-
-    for n, landed in n_hz:
-        wires.arrived(n, landed)
-    total = hz_in[0].astype(F32)
-    for n in range(1, Z):
-        total = total + hz_in[n].astype(F32)
-    head_sum[lo] = total.astype(BF16)
-    n_hp = wires.start(head_sum.at[lo], head_sum.at[lo], y_pair)
 
     for n, landed in n_z:
         wires.arrived(n, landed)
@@ -482,19 +556,20 @@
         src = kv_sum.at[lo, zk(Z - k)]
         wires.arrived(n_zg[k], src)
         n_pair.append((wires.start(src, src, y_pair), kv_sum.at[1 - lo, zk(Z - k)]))
-    wires.arrived(n_hp, head_sum.at[1 - lo])
-    for l in range(2):
-        head_out[l * HALF:(l + 1) * HALF, :] = head_sum[l].astype(F32)
     for n, landed in n_pair:
         wires.arrived(n, landed)
     for l in range(2):
         for b in range(Z):
-            kv_out[l * HALF:(l + 1) * HALF, b * D:(b + 1) * D] = kv_sum[l, b].astype(F32)
+            kv_out[l * HALF:(l + 1) * HALF, b * D:(b + 1) * D] = kv_sum[l, b, :HALF, :].astype(F32)
+        for b in range(5):
+            for v in range(2):
+                rows = kv_sum[l, b, HALF + v * 16:HALF + (v + 1) * 16, :].astype(F32)
+                head_out[l * HALF + b * 16:l * HALF + (b + 1) * 16, v * D:(v + 1) * D] = rows
     wires.drain()
 
 
 def on_device(tokens_in, queries_first, queries_second, teacher_logits, rollout_lengths, send_counts, key_value_weight, head_slice):
-    big = pl.BlockSpec(memory_space=pl.ANY)
+    big = pl.BlockSpec(memory_space=pltpu.HBM)
     small = pl.BlockSpec(memory_space=pltpu.VMEM)
 
     def buf(*shape, dtype=BF16):
@@ -514,14 +589,15 @@
             buf(WIDTH, KV), buf(WIDTH, VOCAB), buf(ROWS, KV),
             buf(2 * HEADS, ROWS, D, dtype=F32), buf(HEADS, ROWS, D),
             buf(ROWS, WIDTH, dtype=F32), buf(ROWS, WIDTH, dtype=F32), buf(ROWS, WIDTH), buf(ROWS, WIDTH),
-            buf(WIDTH, ROWS), buf(WIDTH, ROWS), buf(2 * SHARD, 8 * ROWS), buf(2 * SHARD, 8 * ROWS),
-            buf(8 * ROWS, KV), buf(8 * ROWS, VOCAB), buf(ROWS, WIDTH),
+            buf(WIDTH, ROWS), buf(WIDTH, ROWS), buf(WIDTH, ROWS),
+            buf(2 * SHARD, 8 * ROWS), buf(2 * SHARD, 8 * ROWS), buf(2 * SHARD, 8 * ROWS),
+            buf(8 * ROWS, KV // 2), buf(8 * ROWS, KV // 2 + VOCAB), buf(ROWS, WIDTH),
             buf(256, 15 * D), buf(256, 15 * D),
-            buf(2 * SHARD, KV), buf(3, HALF, KV), buf(Z, HALF, D), buf(Z, HALF, D), buf(2, Z, HALF, D),
-            buf(2 * SHARD, VOCAB), buf(3, HALF, VOCAB), buf(Z, HALF, VOCAB), buf(2, HALF, VOCAB),
+            buf(2 * SHARD, KV // 2), buf(2 * SHARD, KV // 2 + VOCAB), buf(3, HALF, KV // 2), buf(3, HALF, KV // 2 + VOCAB),
+            buf(Z, HALF + 32, D), buf(Z, HALF + 32, D), buf(2, Z, HALF + 32, D),
             pltpu.SemaphoreType.DMA((COPIES,)), pltpu.SemaphoreType.DMA((COPIES,)), pltpu.SemaphoreType.DMA((6,)),
         ],
-        compiler_params=pltpu.CompilerParams(collective_id=0, has_side_effects=True, vmem_limit_bytes=48 * 2**20),
+        compiler_params=pltpu.CompilerParams(collective_id=0, has_side_effects=True, vmem_limit_bytes=60 * 2**20),
         name="pair_backward",
     )(tokens_in, queries_first, queries_second, teacher_logits, rollout_lengths, send_counts, key_value_weight, head_slice)
 

time: 124 us -> 105 us (0.85)
  Pallas kernels: 114 us -> 101 us
  local copies, waits for them, and re-layouts: 9.68 us -> 3.76 us
    pallas_call x1, Pallas kernels: 114 us -> 101 us  [on_device(): pl.pallas_call(kernel, out_shape=(jax.ShapeDtypeStruct((ROWS, WIDTH), BF1...]
    unnamed x19 -> x7, local copies, waits for them, and re-layouts: 9.68 us -> 3.76 us
where the time goes in v3:
time: 105 us
  Pallas kernels  101 us (96%)
  local copies, waits for them, and re-layouts  3.76 us (4%)
    pallas_call x1, Pallas kernels, on_device(): pl.pallas_call(kernel, out_shape=(jax.ShapeDtypeStruct((ROWS, WIDTH), BF1...  101 us
    unnamed x7, local copies, waits for them, and re-layouts  3.76 us

profile of v3, /device:TPU:1, one launch (start us, length us, event | category | flops | bytes accessed | tf_op | source)
XLA Modules:
  0.0 105.1 jit_solution(12761718399651359966)
XLA Ops:
  0.6 100.7 %pair_backward.1 = (bf16[128,2560]{1,0:T(8,128)(2,1)}, f32[160,1024]{1,0:T(8,128)}, f32[160,256]{1,0:T(8,128)}) custom-call(bf16[128,2560]{1,0:T(8,128)(2,1)} %tok_h.1, bf16[128,2560]{1,0:T(8,128)(2,1)} %q1_h.1, bf16[128,2560]{1,0:T(8,128)(2,1)} %q2_h.1, bf16[128,256]{1,0:T(8,128)(2,1)} %tea_h.1, s32[16,1,32]{2,1,0:T(1,128)} %len_ref.1, ...), custom_call_target="tpu_custom_call" | custom-call | tf_op jit(solution)/shard_map/pair_backward/pallas_call | solution.py:578
  101.3 0.0 copy-start
  101.3 2.0 %copy.14 = bf16[128,2560]{1,0:T(8,128)(2,1)} copy(bf16[128,2560]{1,0:T(8,128)(2,1)} %get-tuple-element.6) | data formatting | bytes 1310720
  103.4 0.0 copy-done
  103.4 0.0 copy-start.1
  103.4 0.8 copy.15
  104.2 0.2 copy-done.1
  104.4 0.7 copy.16
Async XLA Ops:
  101.3 2.0 %copy-start = (f32[160,1024]{1,0:T(8,128)S(1)}, f32[160,1024]{1,0:T(8,128)}, u32[]{:S(2)}) copy-start(f32[160,1024]{1,0:T(8,128)} %get-tuple-element.7) | copy-start | bytes 1966084
  103.4 1.1 %copy-start.1 = (f32[160,256]{1,0:T(8,128)S(1)}, f32[160,256]{1,0:T(8,128)}, u32[]{:S(2)}) copy-start(f32[160,256]{1,0:T(8,128)} %get-tuple-element.8) | copy-start | bytes 491524

commit v4 on v3

--- a/solution.py
+++ b/solution.py
@@ -196,9 +196,14 @@
     loads[4].wait()
     n_x, n_far, n_pair = {}, {}, {}
     n_far[0] = to_far(x)
-    for k, half_ in ((1, 1 - lo), (3, 1 - lo), (1, lo), (3, lo), (2, 1 - lo), (2, lo)):
+
+    def send_x(k, half_):
         src = block(hi, x, c, kept, half_)
         n_x.setdefault(k, []).append(wires.start(src, src, at(z, lo, hi, xk(k), c)))
+
+    for half_ in (1 - lo, lo):
+        send_x(1, half_)
+        send_x(3, half_)
     to_core(hi, x, pl.ds(0, KV))
     loads[0].wait()
 
@@ -220,6 +225,8 @@
         return carry
 
     lax.fori_loop(0, 4, transpose_tokens, 0)
+    send_x(2, 1 - lo)
+    send_x(2, lo)
 
     def got_x(k, turn):
         x_ = xk(4 - k)
@@ -311,22 +318,6 @@
 
     got_pair(2)
     n_hfar, n_hcore = gather_far(loads[5], head_full, n_hx)
-    n_hpair = None
-    for i, (n, hi_, x_, half_) in enumerate(w_z):
-        if i == 10:
-            n_hpair = gather_pair(head_full, n_hfar, n_hcore)
-        wires.arrived(n, block(hi_, x_, c, given, half_))
-        to_core(hi_, x_, given, half_)
-    for n, landed in w_core:
-        wires.arrived(n, landed)
-
-    def project(b, carry):
-        cols = pl.ds(pl.multiple_of(b * 256, 256), 256)
-        kv[:, cols] = dot(tok[...], w_full[:, cols]).astype(BF16)
-        return carry
-
-    lax.fori_loop(0, KV // 256, project, 0)
-
     def on_ring(along_x, k, c_):
         if along_x:
             return at(z, lo, hi, xk(k), c_), xk(k) * 2 + c_
@@ -346,6 +337,23 @@
 
     n_tx = exchange_t(tok_tx, tok_x_all, True)
     n_ty = exchange_t(tok_ty, tok_y_all, False)
+
+    n_hpair = None
+    for i, (n, hi_, x_, half_) in enumerate(w_z):
+        if i == 10:
+            n_hpair = gather_pair(head_full, n_hfar, n_hcore)
+        wires.arrived(n, block(hi_, x_, c, given, half_))
+        to_core(hi_, x_, given, half_)
+    for n, landed in w_core:
+        wires.arrived(n, landed)
+
+    def project(b, carry):
+        cols = pl.ds(pl.multiple_of(b * 256, 256), 256)
+        kv[:, cols] = dot(tok[...], w_full[:, cols]).astype(BF16)
+        return carry
+
+    lax.fori_loop(0, KV // 256, project, 0)
+
     loads[1].wait()
     loads[2].wait()
 
@@ -357,15 +365,18 @@
     def attend(j, squares):
         keys = kv[:, lanes(j)]
         values = kv[:, lanes(KV_HEADS + j)]
-        for i in range(PER_KEY):
-            h = j * PER_KEY + i
-            one = softmax_cols(dot_nt(keys, q1[:, lanes(h)]))
-            two = softmax_cols(dot_nt(keys, q2[:, lanes(h)]))
+        heads = [j * PER_KEY + i for i in range(PER_KEY)]
+        scores = [(dot_nt(keys, q1[:, lanes(h)]), dot_nt(keys, q2[:, lanes(h)])) for h in heads]
+        turned = []
+        for h, (s_one, s_two) in zip(heads, scores):
+            one, two = softmax_cols(s_one), softmax_cols(s_two)
             probs[2 * h] = one
             probs[2 * h + 1] = two
             both = (one + two).astype(BF16)
             probs_b[h] = both
-            hid = tok[:, lanes(h)].astype(F32) + dot(both.T, values)
+            turned.append(both.T)
+        for h, both_t in zip(heads, turned):
+            hid = tok[:, lanes(h)].astype(F32) + dot(both_t, values)
             hidden[:, lanes(h)] = hid
             squares = squares + hid * hid
         return squares
@@ -415,8 +426,6 @@
     def wait_all(numbers):
         for n, landed in numbers:
             wires.arrived(n, landed)
-
-    n_gl = ring_send(vals_all, gl_cols, False)
 
     def back_head(b, dots):
         cols = pl.ds(pl.multiple_of(b * 512, 512), 512)
@@ -462,6 +471,7 @@
     kv_cols = pl.ds(0, KV // 2)
     n_keys = ring_send(keys_all, kv_cols, True)
     n_vals = ring_send(vals_all, kv_cols, False)
+    n_gl = ring_send(vals_all, gl_cols, False)
 
     def back_rows(b, carry):
         cols = pl.ds(pl.multiple_of(b * 512, 512), 512)
@@ -482,27 +492,31 @@
         n_rows.append((n, unpack.at[rows_at((g + 16 - k) % 16 * 16, 16)]))
     unpack[rows_at(g * 16, 16), :] = pack[rows_at(g * 16, 16), :]
 
+    n_y = []
+
+    def scatter_x(cols):
+        for k in (1, 3, 2):
+            landed = x_in.at[k - 1, :, cols]
+            n_y.append((wires.start(part_y.at[rows_at(xk(k) * HALF, HALF), cols], landed, on_ring(True, k, c)[0]), landed))
+
     ring_relay(keys_all, kv_cols, True, *n_keys)
-    ring_relay(vals_all, gl_cols, False, *n_gl)
+    ring_relay(vals_all, kv_cols, False, *n_vals)
     wait_all(n_tx)
     wait_all(n_keys[1])
     part_x[...] = dot(tok_x_all[...], keys_all[...]).astype(BF16)
-    n_y = []
     for k in (1, 3, 2):
         hi_, lo_ = yk(k)
         n = wires.start(part_x.at[rows_at(hi_ * SHARD + lo_ * HALF, HALF), :], y_in.at[k - 1], on_ring(False, k, c)[0])
         n_y.append((n, y_in.at[k - 1]))
-
-    ring_relay(vals_all, kv_cols, False, *n_vals)
     wait_all(n_ty)
+    wait_all(n_vals[1])
+    part_y[:, kv_cols] = dot(tok_y_all[...], vals_all[:, kv_cols]).astype(BF16)
+    scatter_x(kv_cols)
+    ring_relay(vals_all, gl_cols, False, *n_gl)
     wait_all(n_norm)
     wait_all(n_gl[1])
-    wait_all(n_vals[1])
-    part_y[:, kv_cols] = dot(tok_y_all[...], vals_all[:, kv_cols]).astype(BF16)
     part_y[:, gl_cols] = dot(norm_y_all[...], vals_all[:, gl_cols]).astype(BF16)
-    for k in (1, 3, 2):
-        n = wires.start(part_y.at[rows_at(xk(k) * HALF, HALF), :], x_in.at[k - 1], on_ring(True, k, c)[0])
-        n_y.append((n, x_in.at[k - 1]))
+    scatter_x(gl_cols)
     own_x = rows_at(hi * SHARD + lo * HALF, HALF)
     own_y = rows_at(x * HALF, HALF)
 

time: 105 us -> 100 us (0.952)
  Pallas kernels: 101 us -> 95.7 us
    pallas_call x1, Pallas kernels: 101 us -> 95.7 us  [on_device(): pl.pallas_call(kernel, out_shape=(jax.ShapeDtypeStruct((ROWS, WIDTH), BF1...]
where the time goes in v4:
time: 100 us
  Pallas kernels  95.7 us (96%)
  local copies, waits for them, and re-layouts  3.76 us (4%)
    pallas_call x1, Pallas kernels, on_device(): pl.pallas_call(kernel, out_shape=(jax.ShapeDtypeStruct((ROWS, WIDTH), BF1...  95.7 us
    unnamed x7, local copies, waits for them, and re-layouts  3.76 us

profile of v4, /device:TPU:1, one launch (start us, length us, event | category | flops | bytes accessed | tf_op | source)
XLA Modules:
  0.0 100.2 jit_solution(746337155208924470)
XLA Ops:
  0.6 95.7 %pair_backward.1 = (bf16[128,2560]{1,0:T(8,128)(2,1)}, f32[160,1024]{1,0:T(8,128)}, f32[160,256]{1,0:T(8,128)}) custom-call(bf16[128,2560]{1,0:T(8,128)(2,1)} %tok_h.1, bf16[128,2560]{1,0:T(8,128)(2,1)} %q1_h.1, bf16[128,2560]{1,0:T(8,128)(2,1)} %q2_h.1, bf16[128,256]{1,0:T(8,128)(2,1)} %tea_h.1, s32[16,1,32]{2,1,0:T(1,128)} %len_ref.1, ...), custom_call_target="tpu_custom_call" | custom-call | tf_op jit(solution)/shard_map/pair_backward/pallas_call | solution.py:592
  96.4 0.0 copy-start
  96.4 2.0 %copy.14 = bf16[128,2560]{1,0:T(8,128)(2,1)} copy(bf16[128,2560]{1,0:T(8,128)(2,1)} %get-tuple-element.6) | data formatting | bytes 1310720
  98.4 0.0 copy-done
  98.4 0.0 copy-start.1
  98.4 0.8 copy.15
  99.3 0.2 copy-done.1
  99.5 0.7 copy.16
Async XLA Ops:
  96.4 2.0 %copy-start = (f32[160,1024]{1,0:T(8,128)S(1)}, f32[160,1024]{1,0:T(8,128)}, u32[]{:S(2)}) copy-start(f32[160,1024]{1,0:T(8,128)} %get-tuple-element.7) | copy-start | bytes 1966084
  98.4 1.1 %copy-start.1 = (f32[160,256]{1,0:T(8,128)S(1)}, f32[160,256]{1,0:T(8,128)}, u32[]{:S(2)}) copy-start(f32[160,256]{1,0:T(8,128)} %get-tuple-element.8) | copy-start | bytes 491524

commit v5 on v4

--- a/solution.py
+++ b/solution.py
@@ -452,16 +452,17 @@
         values = kv[:, lanes(KV_HEADS + j)]
         gk = jnp.zeros((ROWS, D), F32)
         gv = jnp.zeros((ROWS, D), F32)
-        for i in range(PER_KEY):
-            h = j * PER_KEY + i
-            go = grad_o[:, lanes(h)]
-            gp = dot_nt(values, go)
-            gv = gv + dot(probs_b[h], go)
-            for layer, queries in enumerate((q1, q2)):
+        heads = [j * PER_KEY + i for i in range(PER_KEY)]
+        grad_probs = [dot_nt(values, grad_o[:, lanes(h)]) for h in heads]
+        scores = []
+        for h, gp in zip(heads, grad_probs):
+            for layer in range(2):
                 pr = probs[2 * h + layer]
                 along = jnp.sum(pr * gp, axis=0, keepdims=True)
-                gs = (pr * (gp - along) * SCALE).astype(BF16)
-                gk = gk + dot(gs, queries[:, lanes(h)])
+                scores.append((pr * (gp - along) * SCALE).astype(BF16))
+        for i, h in enumerate(heads):
+            gv = gv + dot(probs_b[h], grad_o[:, lanes(h)])
+            gk = gk + dot(scores[2 * i], q1[:, lanes(h)]) + dot(scores[2 * i + 1], q2[:, lanes(h)])
         keys_all[mine_x, lanes(j)] = gk.astype(BF16)
         vals_all[mine_y, lanes(j)] = gv.astype(BF16)
         return carry

time: 100 us -> 100 us (level)
  no operation moved by 1% of the time
where the time goes in v5:
time: 100 us; the launch traced here: 99.7 us
  Pallas kernels  95.2 us (95%)
  local copies, waits for them, and re-layouts  3.76 us (4%)
    pallas_call x1, Pallas kernels, on_device(): pl.pallas_call(kernel, out_shape=(jax.ShapeDtypeStruct((ROWS, WIDTH), BF1...  95.2 us
    unnamed x7, local copies, waits for them, and re-layouts  3.76 us

profile of v5, /device:TPU:1, one launch (start us, length us, event | category | flops | bytes accessed | tf_op | source)
XLA Modules:
  0.0 99.7 jit_solution(16582673461332558524)
XLA Ops:
  0.6 95.2 %pair_backward.1 = (bf16[128,2560]{1,0:T(8,128)(2,1)}, f32[160,1024]{1,0:T(8,128)}, f32[160,256]{1,0:T(8,128)}) custom-call(bf16[128,2560]{1,0:T(8,128)(2,1)} %tok_h.1, bf16[128,2560]{1,0:T(8,128)(2,1)} %q1_h.1, bf16[128,2560]{1,0:T(8,128)(2,1)} %q2_h.1, bf16[128,256]{1,0:T(8,128)(2,1)} %tea_h.1, s32[16,1,32]{2,1,0:T(1,128)} %len_ref.1, ...), custom_call_target="tpu_custom_call" | custom-call | tf_op jit(solution)/shard_map/pair_backward/pallas_call | solution.py:593
  95.9 0.0 copy-start
  95.9 2.0 %copy.14 = bf16[128,2560]{1,0:T(8,128)(2,1)} copy(bf16[128,2560]{1,0:T(8,128)(2,1)} %get-tuple-element.6) | data formatting | bytes 1310720
  97.9 0.0 copy-done
  97.9 0.0 copy-start.1
  97.9 0.8 copy.15
  98.8 0.2 copy-done.1
  99.0 0.7 copy.16
Async XLA Ops:
  95.9 2.0 %copy-start = (f32[160,1024]{1,0:T(8,128)S(1)}, f32[160,1024]{1,0:T(8,128)}, u32[]{:S(2)}) copy-start(f32[160,1024]{1,0:T(8,128)} %get-tuple-element.7) | copy-start | bytes 1966084
  97.9 1.1 %copy-start.1 = (f32[160,256]{1,0:T(8,128)S(1)}, f32[160,256]{1,0:T(8,128)}, u32[]{:S(2)}) copy-start(f32[160,256]{1,0:T(8,128)} %get-tuple-element.8) | copy-start | bytes 491524
